TPU v7x, 128 devices: a whole 4x4x4 slice. The times are simulated.
128 devices in a mesh: dp: 64 (over y, z, x), blk: 2 (over core).
Axes of the slice: x: 4, y: 4, z: 4, core: 2. Of those that a mesh axis runs over, the one named last changes fastest.
Arguments:
- segment: bfloat16 [64, 512, 1024], P('dp', 'blk'), may hold values from -6 to 6
- memory: bfloat16 [64, 384, 1024], P('dp', 'blk'), may hold values from -6 to 6
- compressed: bfloat16 [64, 512, 1024], P('dp', 'blk'), may hold values from -6 to 6
- mem_count: int32 [64], P('dp'), may hold values from 0 to 384, as said below
- comp_count: int32 [64], P('dp'), may hold values from 0 to 512, as said below
- attn_gain: bfloat16 [1024], P(('dp', 'blk')), may hold values from 0.5 to 1.5
- w_query: bfloat16 [1024, 1024], P(('dp', 'blk')), may hold values from -0.1875 to 0.1875
- w_key: bfloat16 [1024, 1024], P(('dp', 'blk')), may hold values from -0.1875 to 0.1875
- w_value: bfloat16 [1024, 1024], P(('dp', 'blk')), may hold values from -0.1875 to 0.1875
- u_bias: bfloat16 [1024], P(('dp', 'blk')), may hold values from -3 to 3
- v_bias: bfloat16 [1024], P(('dp', 'blk')), may hold values from -3 to 3
- w_rel: bfloat16 [1024, 1024], P(('dp', 'blk')), may hold values from -0.1875 to 0.1875
- w_proj: bfloat16 [1024, 1024], P(('dp', 'blk')), may hold values from -1.5 to 1.5
- ffn_gain: bfloat16 [1024], P(('dp', 'blk')), may hold values from 0.5 to 1.5
- w_in: bfloat16 [1024, 4096], P(('dp', 'blk')), may hold values from -0.1875 to 0.1875
- b_in: bfloat16 [4096], P(('dp', 'blk')), may hold values from -3 to 3
- w_out: bfloat16 [4096, 1024], P(('dp', 'blk')), may hold values from -0.09375 to 0.09375
- b_out: bfloat16 [1024], P(('dp', 'blk')), may hold values from -2 to 2
- w_comp: bfloat16 [3072, 1024], P(('dp', 'blk')), may hold values from -0.109375 to 0.109375
- b_comp: bfloat16 [1024], P(('dp', 'blk')), may hold values from -2 to 2
- out_grad: bfloat16 [64, 512, 1024], P('dp', 'blk'), may hold values from -6 to 6
- comp_grad: bfloat16 [64, 128, 1024], P('dp', 'blk'), may hold values from -6 to 6
Outputs:
- output: bfloat16 [64, 512, 1024], P('dp', 'blk')
- new_compressed: bfloat16 [64, 128, 1024], P('dp', 'blk')
- d_segment: float32 [64, 512, 1024], P('dp', 'blk')
- d_attn_gain: float32 [1024], P('blk')
- d_query: float32 [1024, 1024], P('blk')
- d_key: float32 [1024, 1024], P('blk')
- d_value: float32 [1024, 1024], P('blk')
- d_u_bias: float32 [1024], P('blk')
- d_v_bias: float32 [1024], P('blk')
- d_rel: float32 [1024, 1024], P('blk')
- d_proj: float32 [1024, 1024], P('blk')
- d_ffn_gain: float32 [1024], P('blk')
- d_in: float32 [1024, 4096], P('blk')
- d_b_in: float32 [4096], P('blk')
- d_out: float32 [4096, 1024], P('blk')
- d_b_out: float32 [1024], P('blk')
- d_comp: float32 [3072, 1024], P('blk')
- d_b_comp: float32 [1024], P('blk')
Inputs may be any that keep to these rules, and one draw needn't show every extreme that they name: mem_count is the number of valid memory slots of a sequence, which are its last ones; some sequence has all 384. comp_count is the number of valid compressed slots of a sequence, which are its last ones; some sequence has all 512.
All inputs are finite; a program needn't handle non-finite values.
Results may differ from a plain program's by a relative error of at most 0.017.
Values may be sent and summed in bfloat16 or wider, within the bound.
No kernel may reach another device: no remote copies, remote signals or barrier semaphores. Data moves between devices by JAX's collectives and lax.ppermute only.
A program may use at most 256 MiB of HBM per device.

v0:
```python
import math

import jax
import jax.numpy as jnp
from jax import lax
from jax.sharding import PartitionSpec as P

D = 1024
HEAD_DIM = 128
SEG = 512
MEM = 384
COMP = 512
RATE = 3
KTOT = 1408


EPSILON = 1e-05
NEG_FILL = -1e30


def norm_rows(row_vals, gain_vec):
    average = jnp.mean(row_vals, axis=-1, keepdims=True)
    centred = row_vals - average
    variance = jnp.mean(centred * centred, axis=-1, keepdims=True)
    return centred * lax.rsqrt(variance + EPSILON) * gain_vec


def gelu_tanh(inputs):
    return jax.nn.gelu(inputs, approximate=True)


def inner_rows(left_side, right_side):
    return lax.dot_general(
        left_side, right_side, (((0,), (0,)), ((), ())), preferred_element_type=jnp.float32
    )


def times_trans(left_side, right_side):
    return lax.dot_general(
        left_side, right_side, (((1,), (1,)), ((), ())), preferred_element_type=jnp.float32
    )


def sinus_rows(row_total):
    frequency = jnp.exp(jnp.arange(D // 2, dtype=jnp.float32) * (-2.0 * math.log(10000.0) / D))
    distance = jnp.arange(row_total, dtype=jnp.float32)
    angles = distance[:, None] * frequency[None, :]
    return jnp.concatenate([jnp.sin(angles), jnp.cos(angles)], axis=1)


def key_mask(query_pos, mem_valid, comp_valid):
    key_pos = jnp.arange(KTOT, dtype=jnp.int32)
    in_comp = (key_pos < COMP) & (key_pos >= COMP - comp_valid)
    in_mem = (key_pos >= COMP) & (key_pos < COMP + MEM) & (key_pos >= COMP + MEM - mem_valid)
    in_seg = (key_pos[None, :] >= COMP + MEM) & (key_pos[None, :] <= query_pos[:, None])
    return (in_comp | in_mem)[None, :] | in_seg


def skew_rows(wide_pos, key_total):
    head_count, row_count, window_len = wide_pos.shape
    flat_rows = wide_pos.reshape(head_count, row_count * window_len)
    flat_rows = flat_rows[:, row_count - 1 : row_count - 1 + row_count * (window_len - 1)]
    return flat_rows.reshape(head_count, row_count, window_len - 1)[:, :, :key_total]


def skew_back(narrow, window_len):
    head_count, row_count, key_total = narrow.shape
    padded = jnp.pad(narrow, ((0, 0), (0, 0), (0, window_len - 1 - key_total)))
    flat_rows = padded.reshape(head_count, row_count * (window_len - 1))
    flat_rows = jnp.pad(flat_rows, ((0, 0), (row_count - 1, 1)))
    return flat_rows.reshape(head_count, row_count, window_len)


def on_device(
    segment,
    memory,
    compressed,
    mem_count,
    comp_count,
    attn_gain,
    w_query,
    w_key,
    w_value,
    u_bias,
    v_bias,
    w_rel,
    w_proj,
    ffn_gain,
    w_in,
    b_in,
    w_out,
    b_out,
    w_comp,
    b_comp,
    out_grad,
    comp_grad,
):
    gathered = (
        lax.all_gather(attn_gain, ("dp", "blk"), axis=0, tiled=True),
        lax.all_gather(w_query, ("dp", "blk"), axis=0, tiled=True),
        lax.all_gather(w_key, ("dp", "blk"), axis=0, tiled=True),
        lax.all_gather(w_value, ("dp", "blk"), axis=0, tiled=True),
        lax.all_gather(u_bias, ("dp", "blk"), axis=0, tiled=True),
        lax.all_gather(v_bias, ("dp", "blk"), axis=0, tiled=True),
        lax.all_gather(w_rel, ("dp", "blk"), axis=0, tiled=True),
        lax.all_gather(w_proj, ("dp", "blk"), axis=0, tiled=True),
        lax.all_gather(ffn_gain, ("dp", "blk"), axis=0, tiled=True),
        lax.all_gather(w_in, ("dp", "blk"), axis=0, tiled=True),
        lax.all_gather(b_in, ("dp", "blk"), axis=0, tiled=True),
        lax.all_gather(w_out, ("dp", "blk"), axis=0, tiled=True),
        lax.all_gather(b_out, ("dp", "blk"), axis=0, tiled=True),
        lax.all_gather(w_comp, ("dp", "blk"), axis=0, tiled=True),
        lax.all_gather(b_comp, ("dp", "blk"), axis=0, tiled=True),
    )
    (
        gain_attn,
        proj_query,
        proj_key,
        proj_value,
        bias_u,
        bias_v,
        proj_rel,
        proj_out,
        gain_ffn,
        ffn_in,
        ffn_bias,
        ffn_out,
        out_bias,
        comp_proj,
        comp_bias,
    ) = gathered
    seq_count, seg_dev, _ = segment.shape
    mem_dev = memory.shape[1]
    comp_dev = compressed.shape[1]
    cycle_size = lax.axis_size("blk")
    cycle_index = lax.axis_index("blk")
    head_count = D // HEAD_DIM
    window_len = seg_dev + KTOT - 1
    score_scale = 1.0 / math.sqrt(HEAD_DIM)
    edge_two = comp_dev + mem_dev
    local_keys = edge_two + seg_dev
    gain_one = gain_attn.astype(jnp.float32)
    raw_rows = jnp.concatenate([compressed, memory, segment], axis=1).astype(jnp.float32)
    joined = norm_rows(raw_rows, gain_one).astype(jnp.bfloat16)
    flat_joined = joined.reshape(-1, D)
    act_seg = joined[:, edge_two:].reshape(-1, D)
    query_rows = jnp.dot(act_seg, proj_query, preferred_element_type=jnp.float32)
    key_rows = (
        jnp.dot(flat_joined, proj_key, preferred_element_type=jnp.float32)
        .astype(jnp.bfloat16)
        .reshape(seq_count, local_keys, D)
    )
    value_rows = (
        jnp.dot(flat_joined, proj_value, preferred_element_type=jnp.float32)
        .astype(jnp.bfloat16)
        .reshape(seq_count, local_keys, D)
    )
    moved_rows = (
        lax.all_gather(key_rows[:, :comp_dev], "blk", axis=1, tiled=True),
        lax.all_gather(key_rows[:, comp_dev:edge_two], "blk", axis=1, tiled=True),
        lax.all_gather(key_rows[:, edge_two:], "blk", axis=1, tiled=True),
        lax.all_gather(value_rows[:, :comp_dev], "blk", axis=1, tiled=True),
        lax.all_gather(value_rows[:, comp_dev:edge_two], "blk", axis=1, tiled=True),
        lax.all_gather(value_rows[:, edge_two:], "blk", axis=1, tiled=True),
    )
    all_keys = jnp.concatenate([moved_rows[0], moved_rows[1], moved_rows[2]], axis=1).reshape(
        seq_count, KTOT, head_count, HEAD_DIM
    )
    all_values = jnp.concatenate([moved_rows[3], moved_rows[4], moved_rows[5]], axis=1).reshape(
        seq_count, KTOT, head_count, HEAD_DIM
    )
    query_u = (
        (query_rows + bias_u.astype(jnp.float32))
        .astype(jnp.bfloat16)
        .reshape(seq_count, seg_dev, head_count, HEAD_DIM)
    )
    query_v = (
        (query_rows + bias_v.astype(jnp.float32))
        .astype(jnp.bfloat16)
        .reshape(seq_count, seg_dev, head_count, HEAD_DIM)
    )
    pos_table = sinus_rows(KTOT).astype(jnp.bfloat16)
    rel_pos = jnp.dot(pos_table, proj_rel, preferred_element_type=jnp.float32).astype(jnp.bfloat16)
    rel_full = jnp.concatenate([jnp.zeros((SEG, D), jnp.bfloat16), rel_pos], axis=0)
    rel_start = cycle_index * seg_dev + 1
    window = lax.dynamic_slice_in_dim(rel_full, rel_start, window_len, 0)
    rel_rev = window[::-1].reshape(window_len, head_count, HEAD_DIM)
    query_pos = COMP + MEM + cycle_index * seg_dev + jnp.arange(seg_dev, dtype=jnp.int32)

    def scores_for(query_u_one, query_v_one, keys_one, visible):
        content = jnp.einsum(
            "qhd,khd->hqk", query_u_one, keys_one, preferred_element_type=jnp.float32
        )
        wide_pos = jnp.einsum(
            "qhd,lhd->hql", query_v_one, rel_rev, preferred_element_type=jnp.float32
        )
        summed = (content + skew_rows(wide_pos, KTOT)) * score_scale
        return jnp.where(visible[None], summed, NEG_FILL)

    def forward_one(members):
        query_u_one, query_v_one, keys_one, values_one, mem_valid, comp_valid = members
        visible = key_mask(query_pos, mem_valid, comp_valid)
        scores = scores_for(query_u_one, query_v_one, keys_one, visible)
        row_max = jnp.max(scores, axis=-1, keepdims=True)
        shifted = jnp.exp(scores - row_max)
        exp_total = jnp.sum(shifted, axis=-1, keepdims=True)
        prob_low = (shifted / exp_total).astype(jnp.bfloat16)
        mixed_rows = jnp.einsum(
            "hqk,khd->qhd", prob_low, values_one, preferred_element_type=jnp.float32
        )
        return (mixed_rows.astype(jnp.bfloat16), row_max + jnp.log(exp_total))

    attended, log_total = lax.map(
        forward_one, (query_u, query_v, all_keys, all_values, mem_count, comp_count)
    )
    attn_flat = attended.reshape(-1, D)
    seg_rows = raw_rows[:, edge_two:].reshape(-1, D)
    hidden = seg_rows + jnp.dot(attn_flat, proj_out, preferred_element_type=jnp.float32)
    gain_two = gain_ffn.astype(jnp.float32)
    act_two = norm_rows(hidden, gain_two).astype(jnp.bfloat16)
    pre_act = jnp.dot(act_two, ffn_in, preferred_element_type=jnp.float32) + ffn_bias.astype(
        jnp.float32
    )
    activated, gelu_back = jax.vjp(gelu_tanh, pre_act)
    act_ffn = activated.astype(jnp.bfloat16)
    result = (
        hidden
        + jnp.dot(act_ffn, ffn_out, preferred_element_type=jnp.float32)
        + out_bias.astype(jnp.float32)
    )
    output = result.astype(jnp.bfloat16).reshape(segment.shape)
    slot_pos = cycle_index * mem_dev + jnp.arange(mem_dev, dtype=jnp.int32)
    kept_slots = slot_pos[None, :] >= MEM - mem_count[:, None]
    masked = jnp.where(kept_slots[:, :, None], memory, jnp.zeros_like(memory))
    windows = masked.reshape(-1, RATE * D)
    new_compressed = (
        (
            jnp.dot(windows, comp_proj, preferred_element_type=jnp.float32)
            + comp_bias.astype(jnp.float32)
        )
        .astype(jnp.bfloat16)
        .reshape(seq_count, mem_dev // RATE, D)
    )
    (
        gain_attn,
        proj_query,
        proj_key,
        proj_value,
        bias_u,
        bias_v,
        proj_rel,
        proj_out,
        gain_ffn,
        ffn_in,
        ffn_bias,
        ffn_out,
        out_bias,
        comp_proj,
        comp_bias,
    ) = gathered
    gain_one = gain_attn.astype(jnp.float32)
    gain_two = gain_ffn.astype(jnp.float32)
    grad_res = out_grad.reshape(-1, D)
    grad_b_out = jnp.sum(grad_res.astype(jnp.float32), axis=0)
    grad_out = inner_rows(act_ffn, grad_res)
    (grad_pre,) = gelu_back(times_trans(grad_res, ffn_out))
    grad_pre_low = grad_pre.astype(jnp.bfloat16)
    grad_b_in = jnp.sum(grad_pre_low.astype(jnp.float32), axis=0)
    grad_in = inner_rows(act_two, grad_pre_low)
    _, norm_back = jax.vjp(norm_rows, hidden, gain_two)
    grad_hid_norm, grad_gain_two = norm_back(times_trans(grad_pre_low, ffn_in))
    grad_hidden = grad_res.astype(jnp.float32) + grad_hid_norm
    grad_branch = grad_hidden.astype(jnp.bfloat16)
    grad_proj = inner_rows(attn_flat, grad_branch)
    grad_att = (
        times_trans(grad_branch, proj_out)
        .astype(jnp.bfloat16)
        .reshape(seq_count, seg_dev, head_count, HEAD_DIM)
    )

    def backward_one(members):
        query_u_one, query_v_one, keys_one, values_one, mem_valid, comp_valid, log_one, grad_one = (
            members
        )
        visible = key_mask(query_pos, mem_valid, comp_valid)
        scores = scores_for(query_u_one, query_v_one, keys_one, visible)
        probs_full = jnp.exp(scores - log_one)
        prob_low = probs_full.astype(jnp.bfloat16)
        grad_prob = jnp.einsum(
            "qhd,khd->hqk", grad_one, values_one, preferred_element_type=jnp.float32
        )
        inner_sum = jnp.sum(probs_full * grad_prob, axis=-1, keepdims=True)
        grad_score = (probs_full * (grad_prob - inner_sum)).astype(jnp.bfloat16)
        grad_qu = (
            jnp.einsum("hqk,khd->qhd", grad_score, keys_one, preferred_element_type=jnp.float32)
            * score_scale
        )
        grad_keys = (
            jnp.einsum("hqk,qhd->khd", grad_score, query_u_one, preferred_element_type=jnp.float32)
            * score_scale
        )
        grad_values = jnp.einsum(
            "hqk,qhd->khd", prob_low, grad_one, preferred_element_type=jnp.float32
        )
        wide_grad = skew_back(grad_score, window_len)
        grad_qv = (
            jnp.einsum("hql,lhd->qhd", wide_grad, rel_rev, preferred_element_type=jnp.float32)
            * score_scale
        )
        grad_window = (
            jnp.einsum("hql,qhd->lhd", wide_grad, query_v_one, preferred_element_type=jnp.float32)
            * score_scale
        )
        return (grad_qu, grad_qv, grad_keys, grad_values, grad_window)

    grad_qu, grad_qv, grad_keys, grad_values, grad_window = lax.map(
        backward_one,
        (query_u, query_v, all_keys, all_values, mem_count, comp_count, log_total, grad_att),
    )
    grad_u = jnp.sum(grad_qu, axis=(0, 1)).reshape(D)
    grad_v = jnp.sum(grad_qv, axis=(0, 1)).reshape(D)
    grad_query_low = (grad_qu + grad_qv).astype(jnp.bfloat16).reshape(-1, D)
    grad_query = inner_rows(act_seg, grad_query_low)
    keys_flat = grad_keys.reshape(seq_count, KTOT, D)
    values_flat = grad_values.reshape(seq_count, KTOT, D)
    returned = (
        lax.psum_scatter(
            keys_flat[:, :COMP].astype(jnp.bfloat16), "blk", scatter_dimension=1, tiled=True
        ).astype(jnp.float32),
        lax.psum_scatter(
            keys_flat[:, COMP : COMP + MEM].astype(jnp.bfloat16),
            "blk",
            scatter_dimension=1,
            tiled=True,
        ).astype(jnp.float32),
        lax.psum_scatter(
            keys_flat[:, COMP + MEM :].astype(jnp.bfloat16), "blk", scatter_dimension=1, tiled=True
        ).astype(jnp.float32),
        lax.psum_scatter(
            values_flat[:, :COMP].astype(jnp.bfloat16), "blk", scatter_dimension=1, tiled=True
        ).astype(jnp.float32),
        lax.psum_scatter(
            values_flat[:, COMP : COMP + MEM].astype(jnp.bfloat16),
            "blk",
            scatter_dimension=1,
            tiled=True,
        ).astype(jnp.float32),
        lax.psum_scatter(
            values_flat[:, COMP + MEM :].astype(jnp.bfloat16),
            "blk",
            scatter_dimension=1,
            tiled=True,
        ).astype(jnp.float32),
    )
    grad_key_low = (
        jnp.concatenate([returned[0], returned[1], returned[2]], axis=1)
        .astype(jnp.bfloat16)
        .reshape(-1, D)
    )
    grad_value_low = (
        jnp.concatenate([returned[3], returned[4], returned[5]], axis=1)
        .astype(jnp.bfloat16)
        .reshape(-1, D)
    )
    grad_key = inner_rows(flat_joined, grad_key_low)
    grad_value = inner_rows(flat_joined, grad_value_low)
    grad_joined = (
        times_trans(grad_key_low, proj_key) + times_trans(grad_value_low, proj_value)
    ).reshape(seq_count, local_keys, D)
    grad_seg_norm = times_trans(grad_query_low, proj_query).reshape(seq_count, seg_dev, D)
    grad_joined = jnp.concatenate(
        [grad_joined[:, :edge_two], grad_joined[:, edge_two:] + grad_seg_norm], axis=1
    )
    _, first_back = jax.vjp(norm_rows, raw_rows, gain_one)
    grad_raw, grad_gain_one = first_back(grad_joined)
    grad_segment = grad_hidden.reshape(seq_count, seg_dev, D) + grad_raw[:, edge_two:]
    window_sum = jnp.sum(grad_window, axis=0).reshape(window_len, D)[::-1]
    placed = lax.dynamic_update_slice_in_dim(
        jnp.zeros((KTOT + SEG, D), jnp.float32), window_sum, rel_start, 0
    )
    rel_grad = lax.psum(placed[SEG:], ("dp", "blk")).astype(jnp.bfloat16)
    row_share = D // cycle_size
    table_share = lax.dynamic_slice_in_dim(pos_table, cycle_index * row_share, row_share, 1)
    grad_rel = inner_rows(table_share, rel_grad)
    comp_flat = comp_grad.reshape(-1, D)
    grad_comp = inner_rows(windows, comp_flat)
    grad_b_comp = jnp.sum(comp_flat.astype(jnp.float32), axis=0)
    shared = (
        lax.psum_scatter(
            grad_gain_one.astype(jnp.bfloat16), "blk", scatter_dimension=0, tiled=True
        ).astype(jnp.float32),
        lax.psum_scatter(
            grad_query.astype(jnp.bfloat16), "blk", scatter_dimension=0, tiled=True
        ).astype(jnp.float32),
        lax.psum_scatter(
            grad_key.astype(jnp.bfloat16), "blk", scatter_dimension=0, tiled=True
        ).astype(jnp.float32),
        lax.psum_scatter(
            grad_value.astype(jnp.bfloat16), "blk", scatter_dimension=0, tiled=True
        ).astype(jnp.float32),
        lax.psum_scatter(
            grad_u.astype(jnp.bfloat16), "blk", scatter_dimension=0, tiled=True
        ).astype(jnp.float32),
        lax.psum_scatter(
            grad_v.astype(jnp.bfloat16), "blk", scatter_dimension=0, tiled=True
        ).astype(jnp.float32),
        lax.psum_scatter(
            grad_proj.astype(jnp.bfloat16), "blk", scatter_dimension=0, tiled=True
        ).astype(jnp.float32),
        lax.psum_scatter(
            grad_gain_two.astype(jnp.bfloat16), "blk", scatter_dimension=0, tiled=True
        ).astype(jnp.float32),
        lax.psum_scatter(
            grad_in.astype(jnp.bfloat16), "blk", scatter_dimension=0, tiled=True
        ).astype(jnp.float32),
        lax.psum_scatter(
            grad_b_in.astype(jnp.bfloat16), "blk", scatter_dimension=0, tiled=True
        ).astype(jnp.float32),
        lax.psum_scatter(
            grad_out.astype(jnp.bfloat16), "blk", scatter_dimension=0, tiled=True
        ).astype(jnp.float32),
        lax.psum_scatter(
            grad_b_out.astype(jnp.bfloat16), "blk", scatter_dimension=0, tiled=True
        ).astype(jnp.float32),
        lax.psum_scatter(
            grad_comp.astype(jnp.bfloat16), "blk", scatter_dimension=0, tiled=True
        ).astype(jnp.float32),
        lax.psum_scatter(
            grad_b_comp.astype(jnp.bfloat16), "blk", scatter_dimension=0, tiled=True
        ).astype(jnp.float32),
    )
    summed = lax.psum(
        (
            shared[0],
            shared[1],
            shared[2],
            shared[3],
            shared[4],
            shared[5],
            shared[6],
            shared[7],
            shared[8],
            shared[9],
            shared[10],
            shared[11],
            shared[12],
            shared[13],
        ),
        "dp",
    )
    return (
        output,
        new_compressed,
        grad_segment,
        summed[0],
        summed[1],
        summed[2],
        summed[3],
        summed[4],
        summed[5],
        grad_rel,
        summed[6],
        summed[7],
        summed[8],
        summed[9],
        summed[10],
        summed[11],
        summed[12],
        summed[13],
    )


def solution(mesh):
    placed = (
        P("dp", "blk", None),
        P("dp", "blk", None),
        P("dp", "blk", None),
        P("dp"),
        P("dp"),
        P(("dp", "blk")),
        P(("dp", "blk"), None),
        P(("dp", "blk"), None),
        P(("dp", "blk"), None),
        P(("dp", "blk")),
        P(("dp", "blk")),
        P(("dp", "blk"), None),
        P(("dp", "blk"), None),
        P(("dp", "blk")),
        P(("dp", "blk"), None),
        P(("dp", "blk")),
        P(("dp", "blk"), None),
        P(("dp", "blk")),
        P(("dp", "blk"), None),
        P(("dp", "blk")),
        P("dp", "blk", None),
        P("dp", "blk", None),
    )
    return jax.shard_map(
        on_device,
        mesh=mesh,
        in_specs=placed,
        out_specs=(
            P("dp", "blk", None),
            P("dp", "blk", None),
            P("dp", "blk", None),
            P("blk"),
            P("blk", None),
            P("blk", None),
            P("blk", None),
            P("blk"),
            P("blk"),
            P("blk", None),
            P("blk", None),
            P("blk"),
            P("blk", None),
            P("blk"),
            P("blk", None),
            P("blk"),
            P("blk", None),
            P("blk"),
        ),
        check_vma=False,
    )
```

profile of v0, /device:TPU:1, one launch (start us, length us, event | category | flops | bytes accessed | tf_op | source)
XLA Modules:
  0.0 1731.4 jit_solution(10045241930669772750)
XLA Ops:
  16.0 69.2 %all-reduce.18 = (bf16[1024]{0:T(1024)(128)(2,1)S(1)}, bf16[1024]{0:T(1024)(128)(2,1)S(1)}, bf16[1024]{0:T(1024)(128)(2,1)S(1)}, bf16[1024]{0:T(1024)(128)(2,1)}...) all-reduce(bf16[1024]{0:T(1024)(128)(2,1)S(1)} %dynamic-update-slic, ...), channel_id=1, replica_groups=mesh['dp'=64,'blk'=2] {'dp','blk'}, use_global_device_ids=true, to_apply=%add.3 | all-reduce | flops 10240 | bytes 40960
  93.8 52.4 %all-gather.13.cloned.1.call-done = bf16[1024,1024]{1,0:T(8,128)(2,1)} async-done(((bf16[8,1024]{1,0:T(8,128)(2,1)}), bf16[1024,1024]{1,0:T(8,128)(2,1)}) %all-gather.13.cloned.1.call-update) | async-done | bytes 2097168 | tf_op jit(solution)/shard_map/all_gather | solution.py:102
  160.9 12.2 sine_convert_fusion
  173.1 39.0 %all-gather.19.cloned.1.call-done = bf16[1024,1024]{1,0:T(8,128)(2,1)} async-done(((bf16[8,1024]{1,0:T(8,128)(2,1)}), bf16[1024,1024]{1,0:T(8,128)(2,1)}) %all-gather.19.cloned.1.call-update) | async-done | bytes 2097168 | tf_op jit(solution)/shard_map/all_gather | solution.py:100
  216.5 61.3 %all-gather.27.cloned.1.call-done = bf16[1024,1024]{1,0:T(8,128)(2,1)} async-done(((bf16[8,1024]{1,0:T(8,128)(2,1)}), bf16[1024,1024]{1,0:T(8,128)(2,1)}) %all-gather.27.cloned.1.call-update) | async-done | bytes 2097168 | tf_op jit(solution)/shard_map/all_gather | solution.py:105
  277.9 4.9 convolution_convert_fusion.3
  284.4 34.6 %rev.6 = bf16[1663,1024]{1,0:T(8,128)(2,1)} reverse(bf16[1663,1024]{1,0:T(8,128)(2,1)S(1)} %pad_dynamic-slice_fusion), dimensions={0} | reverse | bytes 6811648 | tf_op jit(solution)/shard_map/rev | solution.py:187
  319.0 4.4 copy.85
  323.5 8.2 fusion.78
  331.6 21.5 %reshape.1078 = f32[3405824]{0:T(1024)} reshape(f32[8,256,1663]{2,1,0:T(8,128)} %fusion.78) | data formatting | bytes 27246592
  353.1 13.7 reshape.1032
  366.8 11.0 slice.100
  377.8 10.5 reshape.1080
  388.3 15.6 reshape.1033
  420.4 6.8 fusion.75
  438.3 37.0 %all-gather.31.cloned.1.call-done = bf16[1024,4096]{1,0:T(8,128)(2,1)} async-done(((bf16[8,4096]{1,0:T(8,128)(2,1)}), bf16[1024,4096]{1,0:T(8,128)(2,1)}) %all-gather.31.cloned.1.call-update) | async-done | bytes 8388624 | tf_op jit(solution)/shard_map/all_gather | solution.py:108
  475.3 7.8 convolution_add_fusion
  483.1 62.9 %all-gather.33.cloned.1.call-done = bf16[4096,1024]{1,0:T(8,128)(2,1)} async-done(((bf16[32,1024]{1,0:T(8,128)(2,1)}), bf16[4096,1024]{1,0:T(8,128)(2,1)}) %all-gather.33.cloned.1.call-update) | async-done | bytes 8388624 | tf_op jit(solution)/shard_map/all_gather | solution.py:110
  546.0 12.5 fusion.77
  567.6 10.7 multiply_reduce_fusion
  578.2 6.0 multiply_convert_fusion
  587.6 4.8 copy.76
  597.1 6.8 fusion.15
  604.9 4.8 copy.78
  615.4 4.5 convolution_convert_fusion.2
  620.2 6.1 pad.11
  626.3 13.3 reshape.1082
  639.6 12.9 reshape.1043
  652.5 7.1 pad.12
  659.7 16.3 reshape.1084
  675.9 17.1 reshape.1044
  693.0 5.6 fusion.29
  711.2 5.0 convolution_convert_fusion.7
  718.9 5.0 convolution_convert_fusion.6
  725.2 7.5 convolution_convert_fusion.1
  733.9 8.6 convolution_convert_fusion
  751.5 4.6 fusion.39
  756.2 13.1 reduce-scatter.38.cloned.1.call-done
  769.3 7.1 convolution_multiply_fusion
  776.4 55.3 %reverse = f32[1664,1024]{0,1:T(8,128)} reverse(f32[1664,1024]{0,1:T(8,128)} %bitcast.141), dimensions={0} | reverse | bytes 13631488
  831.6 7.8 slice.132
  843.1 36.3 %dynamic_update_slice.22 = f32[1920,1024]{0,1:T(8,128)} dynamic-update-slice(f32[1920,1024]{0,1:T(8,128)} %broadcast_in_dim.129, f32[1663,1024]{0,1:T(8,128)} %slice.132, s32[]{:T(128)S(6)} %select_n.18, s32[]{:T(128)} %constant.79.clone.1) | dynamic-update-slice | bytes 13623300 | tf_op jit(solution)/shard_map/dynamic_update_slice | solution.py:378
  879.4 6.6 slice.112
  885.9 107.5 %all-reduce.23 = bf16[1408,1024]{0,1:T(8,128)(2,1)} all-reduce(f32[1408,1024]{0,1:T(8,128)} %slice.112), channel_id=1, replica_groups=mesh['dp'=64,'blk'=2] {'dp','blk'}, use_global_device_ids=true, to_apply=%region_32.33 | all-reduce | flops 1441792 | bytes 8650752 | tf_op jit(solution)/shard_map/psum | solution.py:381
  993.4 5.6 fusion.18
  999.0 7.1 fusion.37
  1020.4 5.9 all-reduce.19
  1029.3 695.1 %all-reduce.22 = (f32[512]{0:T(512)}, f32[512,1024]{1,0:T(8,128)}, f32[512,1024]{1,0:T(8,128)}, f32[512,1024]{1,0:T(8,128)}, f32[512]{0:T(512)}, /*index=5*/f32[...) all-reduce(f32[512]{0:T(512)S(1)} %dynamic-slice_convert_fusion.6, ...), channel_id=1, replica_groups=mesh['dp'=64,'blk'=2] {'dp'}, use_global_device_ids=true, to_apply=%region_19.20 | all-reduce | flops 7869440 | bytes 47226880 | tf_op jit(solution)/shard_map/psum | solution.py:432
  (329 shorter events, 133.6 us)
Async XLA Ops:
  7.2 81.4 %copy-start.11 = (bf16[1,256,1024]{2,1,0:T(8,128)(2,1)S(1)}, bf16[1,256,1024]{2,1,0:T(8,128)(2,1)}, u32[]{:S(2)}) copy-start(bf16[1,256,1024]{2,1,0:T(8,128)(2,1)} %param.22) | copy-start | bytes 1572868
  7.2 81.4 %copy-start.6 = (bf16[1,192,1024]{2,1,0:T(8,128)(2,1)S(1)}, bf16[1,192,1024]{2,1,0:T(8,128)(2,1)}, u32[]{:S(2)}) copy-start(bf16[1,192,1024]{2,1,0:T(8,128)(2,1)} %param.23) | copy-start | bytes 1179652
  7.2 81.4 %copy-start.13 = (bf16[1,256,1024]{2,1,0:T(8,128)(2,1)S(1)}, bf16[1,256,1024]{2,1,0:T(8,128)(2,1)}, u32[]{:S(2)}) copy-start(bf16[1,256,1024]{2,1,0:T(8,128)(2,1)} %param.24) | copy-start | bytes 1572868
  7.2 81.4 %all-gather.21.cloned.1.call-start = ((), (), s32[]{:S(2)}) async-start(), calls=%async_computation.17 | async-start | bytes 2113536 | tf_op jit(solution)/shard_map/all_gather | solution.py:101
  8.0 138.2 %all-gather.13.cloned.1.call-start = ((), (), s32[]{:S(2)}) async-start(), calls=%async_computation.13 | async-start | bytes 2113536 | tf_op jit(solution)/shard_map/all_gather | solution.py:102
  8.7 203.4 %all-gather.19.cloned.1.call-start = ((), (), s32[]{:S(2)}) async-start(), calls=%async_computation.16 | async-start | bytes 2113536 | tf_op jit(solution)/shard_map/all_gather | solution.py:100
  9.4 268.4 %all-gather.27.cloned.1.call-start = ((), (), s32[]{:S(2)}) async-start(), calls=%async_computation.20 | async-start | bytes 2113536 | tf_op jit(solution)/shard_map/all_gather | solution.py:105
  10.0 399.1 %all-gather.25.cloned.1.call-start = ((), (), s32[]{:S(2)}) async-start(), calls=%async_computation.19 | async-start | bytes 1572864 | tf_op jit(solution)/shard_map/all_gather | solution.py:161
  85.1 127.0 %copy-start.48 = (f32[1024]{0:T(1024)}, f32[1024]{0:T(1024)S(1)}, u32[]{:S(2)}) copy-start(f32[1024]{0:T(1024)S(1)} %convert_element_type.255) | copy-start | bytes 12292
  86.7 71.1 %copy-start.46 = (f32[704]{0:T(1024)}, f32[704]{0:T(1024)S(1)}, u32[]{:S(2)}) copy-start(f32[704]{0:T(1024)S(1)} %broadcast_multiply_fusion) | copy-start | bytes 8452
  88.6 69.2 %copy-start.50 = (f32[704]{0:T(1024)}, f32[704]{0:T(1024)S(1)}, u32[]{:S(2)}) copy-start(f32[704]{0:T(1024)S(1)} %fusion.58) | copy-start | bytes 8452
  92.0 81.1 %copy-start.35 = (bf16[1,704,1024]{2,1,0:T(8,128)(2,1)}, bf16[1,704,1024]{2,1,0:T(8,128)(2,1)S(1)}, u32[]{:S(2)}) copy-start(bf16[1,704,1024]{2,1,0:T(8,128)(2,1)S(1)} %fusion.24) | copy-start | bytes 4325380
  93.1 315.9 %all-gather.23.cloned.1.call-start = ((), (), s32[]{:S(2)}) async-start(), calls=%async_computation.18 | async-start | bytes 1572864 | tf_op jit(solution)/shard_map/all_gather | solution.py:159
  93.7 322.3 %all-gather.17.cloned.1.call-start = ((), (), s32[]{:S(2)}) async-start(), calls=%async_computation.15 | async-start | bytes 1572864 | tf_op jit(solution)/shard_map/all_gather | solution.py:164
  151.6 264.4 %all-gather.15.cloned.1.call-start = ((), (), s32[]{:S(2)}) async-start(), calls=%async_computation.14 | async-start | bytes 1572864 | tf_op jit(solution)/shard_map/all_gather | solution.py:162
  152.3 282.7 %all-gather.29.cloned.1.call-start = ((), (), s32[]{:S(2)}) async-start(), calls=%async_computation.21 | async-start | bytes 2113536 | tf_op jit(solution)/shard_map/all_gather | solution.py:106
  153.1 322.2 %all-gather.31.cloned.1.call-start = ((), (), s32[]{:S(2)}) async-start(), calls=%async_computation.22 | async-start | bytes 8454144 | tf_op jit(solution)/shard_map/all_gather | solution.py:108
  153.7 392.3 %all-gather.33.cloned.1.call-start = ((), (), s32[]{:S(2)}) async-start(), calls=%async_computation.23 | async-start | bytes 8454144 | tf_op jit(solution)/shard_map/all_gather | solution.py:110
  154.4 553.8 %reduce-scatter.40.cloned.1.call-start = ((), (), s32[]{:S(2)}) async-start(), calls=%async_computation.36 | async-start | bytes 1179648
  173.1 104.8 %copy-start.37 = (bf16[1408,512]{1,0:T(8,128)(2,1)}, bf16[1408,512]{1,0:T(8,128)(2,1)S(1)}, u32[]{:S(2)}) copy-start(bf16[1408,512]{1,0:T(8,128)(2,1)S(1)} %get-tuple-element.148) | copy-start | bytes 4325380
  173.1 104.8 %copy-start.38 = (bf16[1408,512]{1,0:T(8,128)(2,1)S(1)}, bf16[1408,512]{1,0:T(8,128)(2,1)}, u32[]{:S(2)}) copy-start(bf16[1408,512]{1,0:T(8,128)(2,1)} %get-tuple-element.149) | copy-start | bytes 4325380
  388.3 15.6 copy-start.45
  388.3 15.8 slice-start.3
  388.3 18.3 %slice-start.4 = ((bf16[1,704,1024]{2,1,0:T(8,128)(2,1)}), bf16[1,192,1024]{2,1,0:T(8,128)(2,1)S(1)}, s32[]{:S(2)}) async-start(bf16[1,704,1024]{2,1,0:T(8,128)(2,1)} %copy-done.36), calls=%async_computation.42 | async-start | bytes 786432 | tf_op jit(solution)/shard_map/slice | solution.py:163
  437.9 123.6 %copy-start.9 = (f32[256,1024]{1,0:T(8,128)}, f32[256,1024]{1,0:T(8,128)S(1)}, u32[]{:S(2)}) copy-start(f32[256,1024]{1,0:T(8,128)S(1)} %get-tuple-element.153) | copy-start | bytes 3145732
  437.9 123.6 %copy-start.54 = (f32[256]{0:T(256)}, f32[256]{0:T(256)S(1)}, u32[]{:S(2)}) copy-start(f32[256]{0:T(256)S(1)} %broadcast_multiply_fusion.1) | copy-start | bytes 3076
  438.2 123.4 %copy-start.56 = (f32[256]{0:T(256)}, f32[256]{0:T(256)S(1)}, u32[]{:S(2)}) copy-start(f32[256]{0:T(256)S(1)} %fusion.60) | copy-start | bytes 3076
  438.2 107.7 %copy-start.22 = (bf16[1,256,1024]{2,1,0:T(8,128)(2,1)S(1)}, bf16[1,256,1024]{2,1,0:T(8,128)(2,1)}, u32[]{:S(2)}) copy-start(bf16[1,256,1024]{2,1,0:T(8,128)(2,1)} %param.42) | copy-start | bytes 1572868
  546.0 12.5 copy-start.68
  567.5 10.7 slice-start
  567.5 10.7 slice-start.1
  567.6 10.7 slice-start.2
  594.9 116.1 %reduce-scatter.20.cloned.1.call-start = ((), (), s32[]{:S(2)}) async-start(), calls=%async_computation.26 | async-start | bytes 1572864 | tf_op jit(solution)/shard_map/reduce_scatter | solution.py:336
  596.5 114.6 %reduce-scatter.18.cloned.1.call-start = ((), (), s32[]{:S(2)}) async-start(), calls=%async_computation.25 | async-start | bytes 1572864 | tf_op jit(solution)/shard_map/reduce_scatter | solution.py:327
  597.1 119.2 %reduce-scatter.42.cloned.1.call-start = ((), (), s32[]{:S(2)}) async-start(), calls=%async_computation.37 | async-start | bytes 1179648
  612.3 106.6 %reduce-scatter.24.cloned.1.call-start = ((), (), s32[]{:S(2)}) async-start(), calls=%async_computation.28 | async-start | bytes 1572864 | tf_op jit(solution)/shard_map/reduce_scatter | solution.py:348
  613.9 105.0 %reduce-scatter.22.cloned.1.call-start = ((), (), s32[]{:S(2)}) async-start(), calls=%async_computation.27 | async-start | bytes 1572864 | tf_op jit(solution)/shard_map/reduce_scatter | solution.py:339
  614.4 137.1 %all-gather.35.cloned.1.call-start = ((), (), s32[]{:S(2)}) async-start(), calls=%async_computation.24 | async-start | bytes 6340608 | tf_op jit(solution)/shard_map/all_gather | solution.py:112
  615.0 154.3 %reduce-scatter.38.cloned.1.call-start = ((), (), s32[]{:S(2)}) async-start(), calls=%async_computation.35 | async-start | bytes 9437184 | tf_op jit(solution)/shard_map/reduce_scatter | solution.py:425
  620.0 409.3 %reduce-scatter.26.cloned.1.call-start = ((), (), s32[]{:S(2)}) async-start(), calls=%async_computation.29 | async-start | bytes 3145728 | tf_op jit(solution)/shard_map/reduce_scatter | solution.py:392
  675.9 22.7 %copy-start.4 = (bf16[1663,1024]{0,1:T(8,128)(2,1)S(1)}, bf16[1663,1024]{0,1:T(8,128)(2,1)}, u32[]{:S(2)}) copy-start(bf16[1663,1024]{0,1:T(8,128)(2,1)} %copy-done.3) | copy-start | bytes 10217476
  706.0 323.2 %reduce-scatter.32.cloned.1.call-start = ((), (), s32[]{:S(2)}) async-start(), calls=%async_computation.32 | async-start | bytes 3145728 | tf_op jit(solution)/shard_map/reduce_scatter | solution.py:407
  708.2 321.1 %reduce-scatter.28.cloned.1.call-start = ((), (), s32[]{:S(2)}) async-start(), calls=%async_computation.30 | async-start | bytes 3145728 | tf_op jit(solution)/shard_map/reduce_scatter | solution.py:395
  716.2 313.1 %reduce-scatter.30.cloned.1.call-start = ((), (), s32[]{:S(2)}) async-start(), calls=%async_computation.31 | async-start | bytes 3145728 | tf_op jit(solution)/shard_map/reduce_scatter | solution.py:398
  724.0 305.3 %reduce-scatter.34.cloned.1.call-start = ((), (), s32[]{:S(2)}) async-start(), calls=%async_computation.33 | async-start | bytes 12582912 | tf_op jit(solution)/shard_map/reduce_scatter | solution.py:413
  732.7 296.6 %reduce-scatter.36.cloned.1.call-start = ((), (), s32[]{:S(2)}) async-start(), calls=%async_computation.34 | async-start | bytes 12582912 | tf_op jit(solution)/shard_map/reduce_scatter | solution.py:419
  748.3 21.0 %copy-start.19 = (bf16[256,1024]{0,1:T(8,128)(2,1)S(1)}, bf16[256,1024]{0,1:T(8,128)(2,1)}, u32[]{:S(2)}) copy-start(bf16[256,1024]{0,1:T(8,128)(2,1)} %copy.84) | copy-start | bytes 1572868
  1016.5 10.3 copy-start.18
  (58 other events, 229.1 us)
Sparse Core Ops, SparseCore 0:
  11.2 69.0 all-gather.20
  83.4 62.6 all-gather.12
  149.3 62.7 all-gather.18
  215.1 62.7 all-gather.26
  280.0 9.1 all-gather.24
  291.3 13.0 all-gather.22
  306.6 13.0 all-gather.16
  321.9 13.0 all-gather.14
  338.2 66.6 all-gather.28
  407.7 67.5 all-gather.30
  478.3 67.6 all-gather.32
  595.1 8.4 reduce-scatter.39
  606.6 12.5 reduce-scatter.19
  622.0 12.5 reduce-scatter.17
  636.9 12.2 reduce-scatter.41
  651.5 12.5 reduce-scatter.23
  666.4 12.5 reduce-scatter.21
  681.9 69.5 all-gather.34
  754.5 14.7 reduce-scatter.37
  772.2 13.7 reduce-scatter.25
  788.9 13.6 reduce-scatter.31
  805.6 13.6 reduce-scatter.27
  822.2 13.6 reduce-scatter.29
  838.9 20.8 reduce-scatter.33
  862.8 20.8 reduce-scatter.35
where the time goes:
time: 1750 us; the launch traced here: 1730 us
  blocking collectives  883 us (50%)
  local copies, waits for them, and re-layouts  349 us (20%)
  waiting for transfers between devices  277 us (16%)
  matrix products  154 us (9%)
  other arithmetic  49.2 us (3%)
  between operations  18.4 us (1%)
    psum x1, blocking collectives, on_device(): lax.psum((shared[0], shared[1], shared[2], shared[3], shared[4], shared[5...  695 us
    unnamed x188, local copies, waits for them, and re-layouts  164 us
    psum x1, blocking collectives, on_device(): rel_grad = lax.psum(placed[SEG:], ('dp', 'blk')).astype(jnp.bfloat16)  107 us
    unnamed x2, blocking collectives  75.1 us
    all_gather x1, waiting for transfers between devices, on_device(): lax.all_gather(w_out, ('dp', 'blk'), axis=0, tiled=True)  62.9 us
    all_gather x1, waiting for transfers between devices, on_device(): lax.all_gather(w_rel, ('dp', 'blk'), axis=0, tiled=True)  61.3 us
    all_gather x1, waiting for transfers between devices, on_device(): lax.all_gather(w_value, ('dp', 'blk'), axis=0, tiled=True)  52.4 us
    dot_general x8, matrix products, inner_rows(): lax.dot_general(left_side, right_side, (((0,), (0,)), ((), ())), preferre...  41.7 us
  transfers between devices with their start and end apart: 25, of which 7 were waited for; matrix products, arithmetic and copies ran while one was open for 29% of the time, Pallas kernels for 0%

commit v1 on v0

v1 whole, which is shorter than its diff:
```python
import math, functools
import jax, jax.numpy as jnp
from jax import lax
from jax.sharding import PartitionSpec as P
from jax.experimental import pallas as pl
from jax.experimental.pallas import tpu as pltpu
D=1024
FF=4096
HEAD_DIM=128
SEG=512
MEM=384
COMP=512
RATE=3
KTOT=1408
RELN=1536
QB=128
EPSILON=1e-05
SCALE=1.0/math.sqrt(HEAD_DIM); NEG=-1e30
def tdot(a,b):
    return lax.dot_general(a,b,(((1,),(1,)),((),())),preferred_element_type=jnp.float32)
def ndot(a,b):
    return lax.dot_general(a,b,(((1,),(0,)),((),())),preferred_element_type=jnp.float32)
def cdot(a,b):
    return lax.dot_general(a,b,(((0,),(0,)),((),())),preferred_element_type=jnp.float32)

def attn_fwd_kernel(cnt_ref, qu_ref, qv_ref, k_ref, v_ref, r_ref, att_ref, p_ref):
    mc = cnt_ref[0]; cc = cnt_ref[1]
    kp = lax.broadcasted_iota(jnp.int32,(1,COMP+MEM),1)
    ok = ((kp < COMP) & (kp >= COMP-cc)) | ((kp>=COMP)&(kp>=COMP+MEM-mc))
    old_bias = jnp.where(ok, 0.0, NEG)
    tri = jnp.where(lax.broadcasted_iota(jnp.int32,(QB,QB),1) <= lax.broadcasted_iota(jnp.int32,(QB,QB),0), 0.0, NEG)
    for b in range(SEG//QB):
        i0=QB*b; nk=COMP+MEM+QB*(b+1); c0=SEG-QB-QB*b; wl=nk+QB
        s = tdot(qu_ref[pl.ds(i0,QB),:], k_ref[pl.ds(0,nk),:])
        w = tdot(qv_ref[pl.ds(i0,QB),:], r_ref[pl.ds(c0,wl),:])
        w = pltpu.roll(w, wl-(QB-1), 1, stride=1, stride_axis=0)[:,:nk]
        s = (s+w)*SCALE
        parts=[s[:,:COMP+MEM]+old_bias]
        if b: parts.append(s[:,COMP+MEM:nk-QB])
        parts.append(s[:,nk-QB:]+tri)
        s=jnp.concatenate(parts,axis=1)
        m=jnp.max(s,axis=1,keepdims=True)
        e=jnp.exp(s-m)
        l=jnp.sum(e,axis=1,keepdims=True)
        p=(e*(1.0/l)).astype(jnp.bfloat16)
        p_ref[0,pl.ds(i0,QB),pl.ds(0,nk)]=p
        if nk<KTOT: p_ref[0,pl.ds(i0,QB),pl.ds(nk,KTOT-nk)]=jnp.zeros((QB,KTOT-nk),jnp.bfloat16)
        att_ref[pl.ds(i0,QB),:]=ndot(p,v_ref[pl.ds(0,nk),:]).astype(jnp.bfloat16)

def attn_fwd(cnt,qu,qv,k,v,r):
    nh=qu.shape[1]//HEAD_DIM
    col=lambda n: pl.BlockSpec((n,HEAD_DIM),lambda h:(0,h))
    return pl.pallas_call(attn_fwd_kernel, grid=(nh,),
        in_specs=[pl.BlockSpec(memory_space=pltpu.SMEM),col(SEG),col(SEG),col(KTOT),col(KTOT),col(RELN)],
        out_specs=[col(SEG),pl.BlockSpec((1,SEG,KTOT),lambda h:(h,0,0))],
        out_shape=[jax.ShapeDtypeStruct((SEG,nh*HEAD_DIM),jnp.bfloat16),jax.ShapeDtypeStruct((nh,SEG,KTOT),jnp.bfloat16)],
        compiler_params=pltpu.CompilerParams(vmem_limit_bytes=48<<20),
        cost_estimate=pl.CostEstimate(flops=6*nh*SEG*KTOT*HEAD_DIM,bytes_accessed=12<<20,transcendentals=nh*SEG*KTOT),
        name="attention_forward")(cnt,qu,qv,k,v,r)

def attn_bwd_kernel(p_ref, ga_ref, qu_ref, qv_ref, k_ref, v_ref, r_ref, dq_ref, du_ref, dv_ref, dk_ref, dval_ref, dr_ref, ds_s, dw_s, qvr_s):
    flip=((lax.broadcasted_iota(jnp.int32,(QB,QB),0)+lax.broadcasted_iota(jnp.int32,(QB,QB),1))==QB-1).astype(jnp.float32).astype(jnp.bfloat16)
    du=jnp.zeros((1,HEAD_DIM),jnp.float32); dv=du
    for b in range(SEG//QB):
        i0=QB*b; nk=COMP+MEM+QB*(b+1); c0=SEG-QB-QB*b; wl=nk+QB
        rows=pl.ds(i0,QB)
        p=p_ref[0,rows,pl.ds(0,nk)].astype(jnp.float32)
        dp=tdot(ga_ref[rows,:],v_ref[pl.ds(0,nk),:])
        pd=p*dp
        delta=jnp.sum(pd,axis=1,keepdims=True)
        ds=(pd-p*delta).astype(jnp.bfloat16)
        ds_s[rows,pl.ds(0,nk)]=ds
        if nk<KTOT: ds_s[rows,pl.ds(nk,KTOT-nk)]=jnp.zeros((QB,KTOT-nk),jnp.bfloat16)
        wide=jnp.concatenate([ndot(flip,ds),jnp.zeros((QB,QB),jnp.float32)],axis=1)
        wide=pltpu.roll(wide,0,1,stride=1,stride_axis=0).astype(jnp.bfloat16)
        qvr_s[rows,:]=ndot(flip,qv_ref[rows,:]).astype(jnp.bfloat16)
        dw_s[rows,pl.ds(c0,wl)]=wide
        if c0: dw_s[rows,pl.ds(0,c0)]=jnp.zeros((QB,c0),jnp.bfloat16)
        dqu=ndot(ds,k_ref[pl.ds(0,nk),:])*SCALE
        dqr=ndot(wide,r_ref[pl.ds(c0,wl),:])*SCALE
        hi=dqr.astype(jnp.bfloat16); lo=(dqr-hi.astype(jnp.float32)).astype(jnp.bfloat16)
        dqv=ndot(flip,hi)+ndot(flip,lo)
        du+=jnp.sum(dqu,axis=0,keepdims=True); dv+=jnp.sum(dqv,axis=0,keepdims=True)
        dq_ref[rows,:]=(dqu+dqv).astype(jnp.bfloat16)
    du_ref[...]=du; dv_ref[...]=dv
    dk_ref[...]=(cdot(ds_s[...],qu_ref[...])*SCALE).astype(jnp.bfloat16)
    dr_ref[...]=(cdot(dw_s[...],qvr_s[...])*SCALE).astype(jnp.bfloat16)
    dval_ref[...]=cdot(p_ref[0],ga_ref[...]).astype(jnp.bfloat16)

def attn_bwd(p,ga,qu,qv,k,v,r):
    nh=qu.shape[1]//HEAD_DIM
    col=lambda n: pl.BlockSpec((n,HEAD_DIM),lambda h:(0,h))
    sd=lambda n,dt=jnp.bfloat16: jax.ShapeDtypeStruct((n,nh*HEAD_DIM),dt)
    return pl.pallas_call(attn_bwd_kernel, grid=(nh,),
        in_specs=[pl.BlockSpec((1,SEG,KTOT),lambda h:(h,0,0)),col(SEG),col(SEG),col(SEG),col(KTOT),col(KTOT),col(RELN)],
        out_specs=[col(SEG),col(1),col(1),col(KTOT),col(KTOT),col(RELN)],
        out_shape=[sd(SEG),sd(1,jnp.float32),sd(1,jnp.float32),sd(KTOT),sd(KTOT),sd(RELN)],
        scratch_shapes=[pltpu.VMEM((SEG,KTOT),jnp.bfloat16),pltpu.VMEM((SEG,RELN),jnp.bfloat16),pltpu.VMEM((SEG,HEAD_DIM),jnp.bfloat16)],
        compiler_params=pltpu.CompilerParams(vmem_limit_bytes=48<<20),
        cost_estimate=pl.CostEstimate(flops=12*nh*SEG*KTOT*HEAD_DIM,bytes_accessed=20<<20,transcendentals=0),
        name="attention_backward")(p,ga,qu,qv,k,v,r)


ROWS = 136


def swap(array):
    return lax.ppermute(array, "blk", [(0, 1), (1, 0)])


def on_device(
    segment, memory, compressed, mem_count, comp_count, attn_gain, w_query, w_key, w_value, u_bias, v_bias,
    w_rel, w_proj, ffn_gain, w_in, b_in, w_out, b_out, w_comp, b_comp, out_grad, comp_grad,
):
    f32, bf16 = jnp.float32, jnp.bfloat16
    core = lax.axis_index("blk")
    first = core == 0

    def both(own, other, axis=0):
        return jnp.where(first, jnp.concatenate([own, other], axis), jnp.concatenate([other, own], axis))

    def half(array, which, axis):
        size = array.shape[axis] // 2
        return lax.dynamic_slice_in_dim(array, which * size, size, axis)

    vectors = jnp.concatenate([attn_gain, u_bias, v_bias, ffn_gain, b_in, b_out, b_comp])
    vectors = jnp.pad(vectors[None], ((0, 7), (0, D - vectors.shape[0])))
    shard = jnp.concatenate(
        [w_query, w_key, w_value, w_rel, w_proj]
        + [w_in[:, D * c : D * (c + 1)] for c in range(4)]
        + [w_out, w_comp, vectors]
    )
    every = lax.all_gather(shard, ("dp", "blk"), axis=0, tiled=False)

    def columns(at):
        return half(every[:, at : at + 8].reshape(D, D), core, 1)

    proj_query, proj_key, proj_value, proj_rel = (columns(8 * n) for n in range(4))
    proj_out = every[:, 32:40].reshape(D, D)
    ffn_in = [
        lax.dynamic_slice_in_dim(every, 40 + 16 * core + 8 * c, 8, 1).reshape(D, D) for c in range(2)
    ]
    ffn_out = half(every[:, 72:104].reshape(FF, D), core, 0)
    comp_proj = every[:, 104:128].reshape(RATE * D, D)

    def vector(at, size):
        return every[:, 128, at : at + size].reshape(-1).astype(f32)

    gain_one, bias_u, bias_v, gain_two = (vector(8 * n, 8) for n in range(4))
    ffn_bias, out_bias, comp_bias = vector(32, 32), vector(64, 8), vector(72, 8)

    own_rows = jnp.concatenate([compressed[0], memory[0], segment[0], out_grad[0], comp_grad[0]])
    other_rows = swap(own_rows)
    edges = [0, 256, 448, 704, 960, 1024]
    pieces = [both(own_rows[a:b], other_rows[a:b]) for a, b in zip(edges[:-1], edges[1:])]
    raw_rows = jnp.concatenate(pieces[:3]).astype(f32)
    seg_rows = raw_rows[COMP + MEM :]
    grad_res, comp_flat = pieces[3], pieces[4]

    def stats(rows):
        centred = rows - jnp.mean(rows, axis=-1, keepdims=True)
        inverse = lax.rsqrt(jnp.mean(centred * centred, axis=-1, keepdims=True) + EPSILON)
        return centred * inverse, inverse

    normed, inverse = stats(raw_rows)
    joined = (normed * gain_one).astype(bf16)

    distance = (KTOT - 1) - jnp.arange(RELN, dtype=f32)
    frequency = jnp.exp(jnp.arange(D // 2, dtype=f32) * (-2.0 * math.log(10000.0) / D))
    angles = distance[:, None] * frequency[None, :]
    table = jnp.concatenate([jnp.sin(angles), jnp.cos(angles)], axis=1)
    table = jnp.where(distance[:, None] >= 0.0, table, 0.0).astype(bf16)

    slot = jnp.arange(MEM, dtype=jnp.int32)
    masked = jnp.where((slot >= MEM - mem_count[0])[:, None], pieces[1], jnp.zeros_like(pieces[1]))
    windows = masked.reshape(MEM // RATE, RATE * D)
    d_comp = cdot(half(windows, core, 1), comp_flat)
    new_compressed = (ndot(half(windows, core, 0), comp_proj) + comp_bias).astype(bf16)

    query_rows = ndot(joined[COMP + MEM :], proj_query)
    key_rows = ndot(joined, proj_key).astype(bf16)
    value_rows = ndot(joined, proj_value).astype(bf16)
    rel_rows = ndot(table, proj_rel).astype(bf16)
    query_u = (query_rows + half(bias_u, core, 0)).astype(bf16)
    query_v = (query_rows + half(bias_v, core, 0)).astype(bf16)
    counts = jnp.concatenate([mem_count, comp_count])
    attended, probs = attn_fwd(counts, query_u, query_v, key_rows, value_rows, rel_rows)

    hidden = seg_rows + ndot(both(attended, swap(attended), 1), proj_out)
    normed_two, inverse_two = stats(hidden)
    act_two = (normed_two * gain_two).astype(bf16)
    pre_act = jnp.concatenate([ndot(act_two, part) for part in ffn_in], axis=1) + half(ffn_bias, core, 0)
    inner = math.sqrt(2.0 / math.pi)
    tanh = jnp.tanh(inner * (pre_act + 0.044715 * pre_act * pre_act * pre_act))
    act_ffn = (0.5 * pre_act * (1.0 + tanh)).astype(bf16)
    slope = 0.5 * (1.0 + tanh) + (0.5 * inner) * pre_act * (1.0 - tanh * tanh) * (
        1.0 + (3.0 * 0.044715) * pre_act * pre_act
    )
    grad_pre = tdot(grad_res, ffn_out) * slope
    grad_pre = grad_pre.astype(bf16)
    back = tdot(grad_pre, jnp.concatenate(ffn_in, axis=1))
    back = back + swap(back)
    scaled = back * gain_two
    grad_hidden = grad_res.astype(f32) + inverse_two * (
        scaled
        - jnp.mean(scaled, axis=-1, keepdims=True)
        - normed_two * jnp.mean(scaled * normed_two, axis=-1, keepdims=True)
    )
    grad_branch = grad_hidden.astype(bf16)
    grad_att = tdot(grad_branch, half(proj_out, core, 0)).astype(bf16)

    partial = ndot(act_ffn, ffn_out)
    result = half(hidden, core, 0) + half(partial, core, 0) + swap(half(partial, 1 - core, 0)) + out_bias
    output = result.astype(bf16)[None]

    def rows_of(left, right):
        keep = cdot(half(left, core, 1), right)
        send = cdot(half(left, 1 - core, 1), right)
        return keep, send

    def turned(keep, send):
        return both(keep.astype(bf16), swap(send.astype(bf16)), 1)

    d_in = turned(*rows_of(act_two, grad_pre))
    d_out = cdot(act_ffn, grad_res)
    d_proj = cdot(attended, grad_branch)
    early = jnp.concatenate(
        [d_in[:, D * c : D * (c + 1)] for c in range(4)] + [d_out.astype(bf16), d_comp.astype(bf16), d_proj.astype(bf16)]
    )
    early = lax.psum(early, "dp")

    grad_query, d_u, d_v, grad_keys, grad_values, grad_rel = attn_bwd(
        probs, grad_att, query_u, query_v, key_rows, value_rows, rel_rows
    )
    pair_query = rows_of(joined[COMP + MEM :], grad_query)
    pair_key = rows_of(joined, grad_keys)
    pair_value = rows_of(joined, grad_values)
    pair_rel = rows_of(table, grad_rel)

    def gain_share(which, at):
        total = sum(
            jnp.sum(pair[which] * half(weight, at, 0).astype(f32), axis=1)
            for pair, weight in (
                (pair_query, proj_query),
                (pair_key, proj_key),
                (pair_value, proj_value),
            )
        )
        return total / half(gain_one, at, 0)

    d_gain_one = gain_share(0, core) + swap(gain_share(1, 1 - core))
    d_gain_two = jnp.sum(half(back, core, 1) * half(normed_two, core, 1), axis=0)
    d_b_in = jnp.sum(grad_pre.astype(f32), axis=0)
    d_b_out = jnp.sum(half(grad_res, core, 1).astype(f32), axis=0)
    d_b_comp = jnp.sum(half(comp_flat, core, 1).astype(f32), axis=0)
    small = jnp.concatenate([d_gain_one, d_u[0], d_v[0], d_gain_two, d_b_in, d_b_out, d_b_comp])
    small = jnp.pad(small, (0, 8 * D - small.shape[0])).reshape(8, D)
    late = jnp.concatenate(
        [turned(*pair) for pair in (pair_query, pair_key, pair_value, pair_rel)] + [small.astype(bf16)]
    )
    late, early = lax.optimization_barrier((late, early))
    late = lax.psum(late, "dp")

    seg_at = COMP + MEM
    grad_seg = (
        tdot(grad_query, proj_query) + tdot(grad_keys[seg_at:], proj_key) + tdot(grad_values[seg_at:], proj_value)
    )
    grad_seg = half(grad_seg, core, 0) + swap(half(grad_seg, 1 - core, 0))
    scaled_one = grad_seg * gain_one
    normed_seg, inverse_seg = half(normed[seg_at:], core, 0), half(inverse[seg_at:], core, 0)
    d_segment = half(grad_hidden, core, 0) + inverse_seg * (
        scaled_one
        - jnp.mean(scaled_one, axis=-1, keepdims=True)
        - normed_seg * jnp.mean(scaled_one * normed_seg, axis=-1, keepdims=True)
    )

    early, late = early.astype(f32), late.astype(f32)
    d_in = jnp.concatenate([early[512 * c : 512 * (c + 1)] for c in range(4)], axis=1)
    small = late[2048:].reshape(-1)
    return (
        output,
        new_compressed[None],
        d_segment[None],
        small[:512],
        late[:512],
        late[512:1024],
        late[1024:1536],
        small[512:1024],
        small[1024:1536],
        late[1536:2048],
        early[5632:6144],
        small[1536:2048],
        d_in,
        small[2048:4096],
        early[2048:4096],
        small[4096:4608],
        early[4096:5632],
        small[4608:5120],
    )


def solution(mesh):
    rows, weight, vector = P("dp", "blk", None), P(("dp", "blk"), None), P(("dp", "blk"))
    placed = (
        rows, rows, rows, P("dp"), P("dp"), vector, weight, weight, weight, vector, vector,
        weight, weight, vector, weight, vector, weight, vector, weight, vector, rows, rows,
    )
    half_one, half_two = P("blk"), P("blk", None)
    return jax.shard_map(
        on_device,
        mesh=mesh,
        in_specs=placed,
        out_specs=(
            rows, rows, rows, half_one, half_two, half_two, half_two, half_one, half_one,
            half_two, half_two, half_one, half_two, half_one, half_two, half_one, half_two, half_one,
        ),
        check_vma=False,
    )
```

time: 1750 us -> 597 us (0.34)
  blocking collectives: 883 us -> 0 us
  local copies, waits for them, and re-layouts: 349 us -> 113 us
  matrix products: 154 us -> 72.1 us
  Pallas kernels: 0 us -> 35.9 us
    psum x2 -> x0, blocking collectives: 803 us -> none  [the longest x1 695 us: on_device(): lax.psum((shared[0], shared[1], shared[2], shared[3], shared[4], shared[5...]
    psum x0 -> x2, waiting for transfers between devices: none -> 192 us  [the longest x1 101 us: on_device(): late = lax.psum(late, 'dp')]
    all_gather x12 -> x1, waiting for transfers between devices: 256 us -> 85.9 us  [on_device(): every = lax.all_gather(shard, ('dp', 'blk'), axis=0, tiled=False)]
    unnamed x188 -> x187, local copies, waits for them, and re-layouts: 164 us -> 38.4 us
    dot_general x31 -> x28, matrix products: 154 us -> 72.1 us  [the longest x13 34.8 us: cdot(): lax.dot_general(a, b, (((0,), (0,)), ((), ())), preferred_element_type=jn...]
    unnamed x2 -> x0, blocking collectives: 75.1 us -> none
    reshape x6 -> x1, local copies, waits for them, and re-layouts: 63.9 us -> 10.2 us  [on_device(): proj_out = every[:, 32:40].reshape(D, D)]
    dynamic_update_slice x1 -> x0, local copies, waits for them, and re-layouts: 36.3 us -> none  [on_device(): lax.dynamic_update_slice_in_dim(jnp.zeros((KTOT + SEG, D), jnp.float32),...]
  transfers between devices with their start and end apart: 25 -> 14, of which waited for: 7 -> 3; matrix products, arithmetic and copies ran while one was open for 29% -> 27% of each run, Pallas kernels for 0% -> 4%
where the time goes in v1:
time: 597 us; the launch traced here: 587 us
  waiting for transfers between devices  278 us (47%)
  local copies, waits for them, and re-layouts  113 us (19%)
  matrix products  72.1 us (12%)
  other arithmetic  66 us (11%)
  Pallas kernels  35.9 us (6%)
  between operations  16.2 us (3%)
  starting transfers between devices  6.68 us (1%)
    psum x1, waiting for transfers between devices, on_device(): late = lax.psum(late, 'dp')  101 us
    psum x1, waiting for transfers between devices, on_device(): early = lax.psum(early, 'dp')  90.8 us
    all_gather x1, waiting for transfers between devices, on_device(): every = lax.all_gather(shard, ('dp', 'blk'), axis=0, tiled=False)  85.9 us
    unnamed x187, local copies, waits for them, and re-layouts  38.4 us
    dot_general x13, matrix products, cdot(): lax.dot_general(a, b, (((0,), (0,)), ((), ())), preferred_element_type=jn...  34.8 us
    dot_general x9, matrix products, ndot(): lax.dot_general(a, b, (((1,), (0,)), ((), ())), preferred_element_type=jn...  23.5 us
    pallas_call x1, Pallas kernels, attn_bwd(): pl.pallas_call(attn_bwd_kernel, grid=(nh,), in_specs=[pl.BlockSpec((1, SE...  22 us
    pallas_call x1, Pallas kernels, attn_fwd(): pl.pallas_call(attn_fwd_kernel, grid=(nh,), in_specs=[pl.BlockSpec(memory...  13.9 us
  transfers between devices with their start and end apart: 14, of which 3 were waited for; matrix products, arithmetic and copies ran while one was open for 27% of the time, Pallas kernels for 4%

profile of v1, /device:TPU:1, one launch (start us, length us, event | category | flops | bytes accessed | tf_op | source)
XLA Modules:
  0.0 587.0 jit_solution(6432545131604854175)
XLA Ops:
  15.5 4.8 concatenate.112
  28.8 11.9 %multiply_sine_fusion = (bf16[1536,512]{1,0:T(8,128)(2,1)S(1)}, bf16[1536,512]{1,0:T(8,128)(2,1)S(1)}) fusion(f32[512]{0:T(512)S(1)} %multiply_exponential_fusion, f32[1536]{0:T(1024)S(1)} %iota_subtract_fusion), kind=kLoop, calls=%fused_computation.9 | loop fusion | flops 2359296 | bytes 3153920 | tf_op jit(solution)/shard_map/sin | solution.py:171
  40.8 2.3 fusion
  48.7 85.9 %all-gather.3.cloned.1.call-done = bf16[17408,1024]{1,0:T(8,128)(2,1)} async-done(((bf16[136,1024]{1,0:T(8,128)(2,1)}), bf16[17408,1024]{1,0:T(8,128)(2,1)}) %all-gather.3.cloned.1.call-update) | async-done | bytes 35651600 | tf_op jit(solution)/shard_map/all_gather | solution.py:133
  134.6 3.9 fusion.74
  138.9 4.3 subtract_multiply_fusion
  143.3 10.2 %slice_bitcast_fusion = (bf16[1024,1024]{1,0:T(8,128)(2,1)}, bf16[1024,1024]{1,0:T(8,128)(2,1)}, bf16[1024,1024]{1,0:T(8,128)(2,1)}, bf16[1024,1024]{1,0:T(8,128...) fusion(bf16[128,136,1024]{2,1,0:T(8,128)(2,1)} %bitcast.78, ...), kind=kLoop, calls=%fused_computation.38 | loop fusion | bytes 29360136 | tf_op jit(solution)/shard_map/reshape | solution.py:139
  160.8 13.9 %attention_forward.1 = (bf16[512,512]{1,0:T(8,128)(2,1)S(1)}, bf16[4,512,1408]{2,1,0:T(8,128)(2,1)}) custom-call(s32[2]{0:T(128)S(1)} %pad_add_fusion.cnt_ref, bf16[512,512]{1,0:T(8,128)(2,1)S(1)} %get-tuple-element.80.qu_ref, bf16[512,512]{1,0:T(8,128)(2,1)S(1)} %get-tuple-element.79.qv_ref, bf16[1408,512]{1,0:T(8,128)(2,1)S(1)} %convolution_convert_fusion.5.k_ref, ...), custom_call_target="tpu_custom_call" | custom-call | flops 2214592512 | bytes 12582912 | tf_op jit(solution)/shard_map/attention_forward/pallas_call | solution.py:53
  175.3 3.1 fusion.106
  178.5 8.7 %slice.230 = bf16[128,32,1024]{2,1,0:T(8,128)(2,1)} slice(bf16[128,136,1024]{2,1,0:T(8,128)(2,1)} %bitcast.79), slice={[0:128], [72:104], [0:1024]} | slice | bytes 16777216 | tf_op jit(solution)/shard_map/slice | solution.py:143
  188.5 3.9 fusion.115
  196.3 2.1 copy-done.37
  200.2 5.7 fusion.116
  206.0 3.7 fusion.8
  209.9 4.4 convolution_convert_fusion.1
  220.3 3.0 convolution_convert_fusion.2
  223.3 2.8 multiply_reduce_fusion.3
  226.1 3.9 maximum_select_fusion.1
  234.9 5.2 convert_dynamic-update-slice_fusion
  240.7 2.6 fusion.12
  246.6 2.3 slice.220
  252.9 3.5 fusion.110
  256.4 2.2 copy.66
  258.6 2.1 copy.69
  262.7 6.0 %fusion.15 = f32[512,1024]{1,0:T(8,128)S(1)} fusion(bf16[4096,1024]{1,0:T(8,128)(2,1)} %bitcast.83, s32[]{:T(128)S(6)} %select_n.149, f32[512,1024]{1,0:T(8,128)S(1)} %copy-done.68, f32[512,1024]{1,0:T(8,128)} %copy-done.69, f32[2048]{0:T(1024)S(1)} %copy-done.63), kind=kOutput, calls=%fused_computation.30 | convolution fusion | flops 2159017984 | bytes 10493956 | tf_op jit(solution)/shard_map/dot_general | solution.py:22
  272.4 22.0 %attention_backward.1 = (bf16[512,512]{1,0:T(8,128)(2,1)S(1)}, f32[1,512]{1,0:T(1,128)S(1)}, f32[1,512]{1,0:T(1,128)S(1)}, bf16[1408,512]{1,0:T(8,128)(2,1)S(1)}...) custom-call(bf16[4,512,1408]{2,1,0:T(8,128)(2,1)} %get-tuple-element.29.p_ref, ...), custom_call_target="tpu_custom_call" | custom-call | flops 4429185024 | bytes 20971520 | tf_op jit(solution)/shard_map/attention_backward/pallas_call | solution.py:94
  298.3 2.8 multiply_reduce_fusion.7
  303.6 2.5 multiply_reduce_fusion.10
  306.1 3.4 fusion.24
  318.0 2.1 copy.56
  320.1 2.1 copy.55
  322.2 2.1 copy.53
  328.2 2.9 fusion.45
  331.1 2.6 fusion.46
  333.7 2.6 fusion.47
  336.2 2.5 fusion.48
  339.4 90.8 %all-reduce.5.cloned.1.call-done = bf16[6144,1024]{1,0:T(8,128)(2,1)} async-done(((bf16[6144,1024]{1,0:T(8,128)(2,1)}), bf16[6144,1024]{1,0:T(8,128)(2,1)}) %all-reduce.5.cloned.1.call-update) | async-done | bytes 12582928 | tf_op jit(solution)/shard_map/psum | solution.py:230
  430.2 2.1 fusion.57
  437.4 6.5 %slice.232 = bf16[128,24,1024]{2,1,0:T(8,128)(2,1)} slice(bf16[128,136,1024]{2,1,0:T(8,128)(2,1)} %bitcast.82), slice={[0:128], [104:128], [0:1024]} | slice | bytes 12582912 | tf_op jit(solution)/shard_map/slice | solution.py:144
  446.0 5.2 fusion.39
  451.2 2.8 fusion.62
  457.0 3.4 slice.259
  460.5 4.4 slice.257
  464.9 2.7 fusion.108
  467.6 3.7 pad_maximum_fusion
  471.3 100.8 %all-reduce.7.cloned.1.call-done = bf16[2056,1024]{1,0:T(8,128)(2,1)} async-done(((bf16[2056,1024]{1,0:T(8,128)(2,1)}), bf16[2056,1024]{1,0:T(8,128)(2,1)}) %all-reduce.7.cloned.1.call-update) | async-done | bytes 4210704 | tf_op jit(solution)/shard_map/psum | solution.py:262
  572.0 3.4 convert_element_type.239
  576.7 3.6 fusion.109
  (295 shorter events, 91.7 us)
Async XLA Ops:
  7.2 15.7 %copy-start.48 = (bf16[1,192,1024]{2,1,0:T(8,128)(2,1)S(1)}, bf16[1,192,1024]{2,1,0:T(8,128)(2,1)}, u32[]{:S(2)}) copy-start(bf16[1,192,1024]{2,1,0:T(8,128)(2,1)} %param.23) | copy-start | bytes 1179652
  7.2 16.5 %copy-start.41 = (bf16[1,256,1024]{2,1,0:T(8,128)(2,1)S(1)}, bf16[1,256,1024]{2,1,0:T(8,128)(2,1)}, u32[]{:S(2)}) copy-start(bf16[1,256,1024]{2,1,0:T(8,128)(2,1)} %param.22) | copy-start | bytes 1572868
  7.2 17.3 %copy-start.39 = (bf16[1,256,1024]{2,1,0:T(8,128)(2,1)S(1)}, bf16[1,256,1024]{2,1,0:T(8,128)(2,1)}, u32[]{:S(2)}) copy-start(bf16[1,256,1024]{2,1,0:T(8,128)(2,1)} %param.42) | copy-start | bytes 1572868
  7.2 127.3 %all-gather.3.cloned.1.call-start = ((), (), s32[]{:S(2)}) async-start(), calls=%async_computation.2 | async-start | bytes 35930112 | tf_op jit(solution)/shard_map/all_gather | solution.py:133
  20.3 5.1 copy-start.52
  21.0 409.2 %all-reduce.5.cloned.1.call-start = ((), (), s32[]{:S(2)}) async-start(), calls=%async_computation | async-start | bytes 25165824 | tf_op jit(solution)/shard_map/psum | solution.py:230
  26.0 17.0 %collective-permute-start = (bf16[1024,1024]{1,0:T(8,128)(2,1)}, bf16[1024,1024]{1,0:T(8,128)(2,1)S(1)}, u32[]{:S(2)}, u32[]{:S(2)}) collective-permute-start(bf16[1024,1024]{1,0:T(8,128)(2,1)} %constant_dynamic-update-slice_fusion), channel_id=1, source_target_pairs={{0,1},{1,0},{2,3},{3,2},{4,5},{5,4},{6,7},{7,6},{8,9},{9,8},{10,11... | collective-permute-start | bytes 6291464 | tf_op jit(solution)/shard_map/ppermute | solution.py:108
  143.3 16.4 %copy-start.29 = (bf16[1408,1024]{1,0:T(8,128)(2,1)}, bf16[1408,1024]{1,0:T(8,128)(2,1)S(1)}, u32[]{:S(2)}) copy-start(bf16[1408,1024]{1,0:T(8,128)(2,1)S(1)} %get-tuple-element.69) | copy-start | bytes 8650756
  153.5 6.2 %copy-start.22 = (bf16[1024,1024]{1,0:T(8,128)(2,1)}, bf16[1024,1024]{1,0:T(8,128)(2,1)S(1)}, u32[]{:S(2)}) copy-start(bf16[1024,1024]{1,0:T(8,128)(2,1)S(1)} %get-tuple-element.58) | copy-start | bytes 6291460
  155.2 5.3 copy-start.1
  160.4 14.3 %copy-start.3 = (bf16[512,512]{1,0:T(8,128)(2,1)}, bf16[512,512]{1,0:T(8,128)(2,1)S(1)}, u32[]{:S(2)}) copy-start(bf16[512,512]{1,0:T(8,128)(2,1)S(1)} %get-tuple-element.79.qv_ref) | copy-start | bytes 1572868
  160.4 14.3 %copy-start.5 = (bf16[512,512]{1,0:T(8,128)(2,1)}, bf16[512,512]{1,0:T(8,128)(2,1)S(1)}, u32[]{:S(2)}) copy-start(bf16[512,512]{1,0:T(8,128)(2,1)S(1)} %get-tuple-element.80.qu_ref) | copy-start | bytes 1572868
  174.7 13.8 %collective-permute-start.1 = (bf16[512,512]{1,0:T(8,128)(2,1)S(1)}, bf16[512,512]{1,0:T(8,128)(2,1)}, u32[]{:S(2)}, u32[]{:S(2)}) collective-permute-start(bf16[512,512]{1,0:T(8,128)(2,1)S(1)} %get-tuple-element.28), channel_id=1, source_target_pairs={{0,1},{1,0},{2,3},{3,2},{4,5},{5,4},{6,7},{7,6},{8,9},{9,8},{10,11... | collective-permute-start | bytes 1572872 | tf_op jit(solution)/shard_map/ppermute | solution.py:108
  188.5 11.2 %copy-start.62 = (f32[2048]{0:T(1024)}, f32[2048]{0:T(1024)S(1)}, u32[]{:S(2)}) copy-start(f32[2048]{0:T(1024)S(1)} %dynamic_slice.132) | copy-start | bytes 24580
  192.8 6.9 %slice-start.3 = ((s8[8388608]{0:T(1024)(128)(4,1)}), s8[4194304]{0:T(1024)(128)(4,1)S(1)}, s32[]{:S(2)}) async-start(s8[8388608]{0:T(1024)(128)(4,1)} %bitcast.84), calls=%async_computation.6 | async-start | bytes 8388608
  193.8 46.3 %copy-start.8 = (f32[512,1024]{1,0:T(8,128)}, f32[512,1024]{1,0:T(8,128)S(1)}, u32[]{:S(2)}) copy-start(f32[512,1024]{1,0:T(8,128)S(1)} %get-tuple-element.51) | copy-start | bytes 6291460
  195.0 4.8 slice-start.4
  199.7 6.3 %copy-start.69 = (f32[512,1024]{1,0:T(8,128)}, f32[512,1024]{1,0:T(8,128)S(1)}, u32[]{:S(2)}) copy-start(f32[512,1024]{1,0:T(8,128)S(1)} %fusion.117) | copy-start | bytes 6291460
  209.7 13.6 %collective-permute-start.3 = (f32[512,1024]{1,0:T(8,128)}, f32[512,1024]{1,0:T(8,128)}, u32[]{:S(2)}, u32[]{:S(2)}) collective-permute-start(f32[512,1024]{1,0:T(8,128)} %fusion.8), channel_id=1, source_target_pairs={{0,1},{1,0},{2,3},{3,2},{4,5},{5,4},{6,7},{7,6},{8,9},{9,8},{10,11... | collective-permute-start | bytes 6291464 | tf_op jit(solution)/shard_map/ppermute | solution.py:108
  214.3 11.7 %collective-permute-start.10 = (bf16[512,2048]{1,0:T(8,128)(2,1)}, bf16[512,2048]{1,0:T(8,128)(2,1)}, u32[]{:S(2)}, u32[]{:S(2)}) collective-permute-start(bf16[512,2048]{1,0:T(8,128)(2,1)} %convolution_convert_fusion.1), channel_id=1, source_target_pairs={{0,1},{1,0},{2,3},{3,2},{4,5},{5,4},{6,7},{7,6},{8,9},{9,8},{10,11... | collective-permute-start | bytes 6291464 | tf_op jit(solution)/shard_map/ppermute | solution.py:108
  218.9 21.8 %copy-start.32 = (bf16[128,3072]{0,1:T(8,128)(2,1)}, bf16[128,3072]{0,1:T(8,128)(2,1)S(1)}, u32[]{:S(2)}) copy-start(bf16[128,3072]{0,1:T(8,128)(2,1)S(1)} %bitcast_select_fusion) | copy-start | bytes 2359300
  220.3 20.5 %copy-start.46 = (bf16[128,1024]{1,0:T(8,128)(2,1)}, bf16[128,1024]{1,0:T(8,128)(2,1)S(1)}, u32[]{:S(2)}) copy-start(bf16[128,1024]{1,0:T(8,128)(2,1)S(1)} %maximum_select_fusion.12) | copy-start | bytes 786436
  226.0 14.1 %copy-start.13 = (f32[512,1024]{1,0:T(8,128)}, f32[512,1024]{1,0:T(8,128)S(1)}, u32[]{:S(2)}) copy-start(f32[512,1024]{1,0:T(8,128)S(1)} %get-tuple-element.49) | copy-start | bytes 6291460
  234.9 5.2 copy-start.61
  245.2 326.9 %all-reduce.7.cloned.1.call-start = ((), (), s32[]{:S(2)}) async-start(), calls=%async_computation.1 | async-start | bytes 8421376 | tf_op jit(solution)/shard_map/psum | solution.py:262
  248.9 4.0 copy-start.20
  256.4 6.3 %copy-start.68 = (f32[512,1024]{1,0:T(8,128)S(1)}, f32[512,1024]{1,0:T(8,128)}, u32[]{:S(2)}) copy-start(f32[512,1024]{1,0:T(8,128)} %copy-done.66) | copy-start | bytes 6291460
  262.7 7.7 %copy-start.34 = (bf16[1024,1024]{1,0:T(8,128)(2,1)S(1)}, bf16[1024,1024]{1,0:T(8,128)(2,1)}, u32[]{:S(2)}) copy-start(bf16[1024,1024]{1,0:T(8,128)(2,1)} %get-tuple-element.52) | copy-start | bytes 6291460
  269.8 181.4 %collective-permute-start.2 = (f32[256,1024]{1,0:T(8,128)}, f32[256,1024]{1,0:T(8,128)}, u32[]{:S(2)}, u32[]{:S(2)}) collective-permute-start(f32[256,1024]{1,0:T(8,128)} %constant_dynamic-slice_fusion.1), channel_id=1, source_target_pairs={{0,1},{1,0},{2,3},{3,2},{4,5},{5,4},{6,7},{7,6},{8,9},{9,8},{10,11... | collective-permute-start | bytes 3145736 | tf_op jit(solution)/shard_map/ppermute | solution.py:108
  272.4 22.0 %copy-start.30 = (bf16[1408,1024]{1,0:T(8,128)(2,1)S(1)}, bf16[1408,1024]{1,0:T(8,128)(2,1)}, u32[]{:S(2)}) copy-start(bf16[1408,1024]{1,0:T(8,128)(2,1)} %copy-done.29) | copy-start | bytes 8650756
  272.4 22.0 %copy-start.56 = (bf16[512,512]{0,1:T(8,128)(2,1)S(1)}, bf16[512,512]{0,1:T(8,128)(2,1)}, u32[]{:S(2)}) copy-start(bf16[512,512]{0,1:T(8,128)(2,1)} %copy.69) | copy-start | bytes 1572868
  303.1 25.1 %collective-permute-start.5 = (bf16[512,512]{1,0:T(8,128)(2,1)}, bf16[512,512]{1,0:T(8,128)(2,1)}, u32[]{:S(2)}, u32[]{:S(2)}) collective-permute-start(bf16[512,512]{1,0:T(8,128)(2,1)} %copy.52), channel_id=1, source_target_pairs={{0,1},{1,0},{2,3},{3,2},{4,5},{5,4},{6,7},{7,6},{8,9},{9,8},{10,11... | collective-permute-start | bytes 1572872 | tf_op jit(solution)/shard_map/ppermute | solution.py:108
  303.1 28.0 %collective-permute-start.6 = (bf16[512,512]{1,0:T(8,128)(2,1)}, bf16[512,512]{1,0:T(8,128)(2,1)}, u32[]{:S(2)}, u32[]{:S(2)}) collective-permute-start(bf16[512,512]{1,0:T(8,128)(2,1)} %copy.54), channel_id=1, source_target_pairs={{0,1},{1,0},{2,3},{3,2},{4,5},{5,4},{6,7},{7,6},{8,9},{9,8},{10,11... | collective-permute-start | bytes 1572872 | tf_op jit(solution)/shard_map/ppermute | solution.py:108
  317.3 9.4 %collective-permute-start.9 = (f32[512]{0:T(512)S(1)}, f32[512]{0:T(512)S(1)}, u32[]{:S(2)}, u32[]{:S(2)}) collective-permute-start(f32[512]{0:T(512)S(1)} %dynamic-slice_divide_fusion), channel_id=1, source_target_pairs={{0,1},{1,0},{2,3},{3,2},{4,5},{5,4},{6,7},{7,6},{8,9},{9,8},{10,11... | collective-permute-start | bytes 6152 | tf_op jit(solution)/shard_map/ppermute | solution.py:108
  318.0 9.7 %copy-start.64 = (bf16[2048]{0:T(1024)(128)(2,1)S(1)}, bf16[2048]{0:T(1024)(128)(2,1)}, u32[]{:S(2)}) copy-start(bf16[2048]{0:T(1024)(128)(2,1)} %get-tuple-element.103) | copy-start | bytes 12292
  326.3 7.4 %collective-permute-start.7 = (bf16[512,512]{1,0:T(8,128)(2,1)}, bf16[512,512]{1,0:T(8,128)(2,1)}, u32[]{:S(2)}, u32[]{:S(2)}) collective-permute-start(bf16[512,512]{1,0:T(8,128)(2,1)} %copy.56), channel_id=1, source_target_pairs={{0,1},{1,0},{2,3},{3,2},{4,5},{5,4},{6,7},{7,6},{8,9},{9,8},{10,11... | collective-permute-start | bytes 1572872 | tf_op jit(solution)/shard_map/ppermute | solution.py:108
  326.7 9.6 %collective-permute-start.8 = (bf16[512,512]{1,0:T(8,128)(2,1)}, bf16[512,512]{1,0:T(8,128)(2,1)}, u32[]{:S(2)}, u32[]{:S(2)}) collective-permute-start(bf16[512,512]{1,0:T(8,128)(2,1)} %fusion.27), channel_id=1, source_target_pairs={{0,1},{1,0},{2,3},{3,2},{4,5},{5,4},{6,7},{7,6},{8,9},{9,8},{10,11... | collective-permute-start | bytes 1572872 | tf_op jit(solution)/shard_map/ppermute | solution.py:108
  328.1 5.5 copy-start.43
  331.1 5.2 copy-start.45
  435.7 18.3 %collective-permute-start.4 = (f32[256,1024]{1,0:T(8,128)}, f32[256,1024]{1,0:T(8,128)}, u32[]{:S(2)}, u32[]{:S(2)}) collective-permute-start(f32[256,1024]{1,0:T(8,128)} %constant_dynamic-slice_fusion), channel_id=1, source_target_pairs={{0,1},{1,0},{2,3},{3,2},{4,5},{5,4},{6,7},{7,6},{8,9},{9,8},{10,11... | collective-permute-start | bytes 3145736 | tf_op jit(solution)/shard_map/ppermute | solution.py:108
  437.4 6.5 %copy-start.59 = (f32[128,8]{1,0:T(8,128)S(1)}, f32[128,8]{1,0:T(8,128)}, u32[]{:S(2)}) copy-start(f32[128,8]{1,0:T(8,128)} %get-tuple-element.38) | copy-start | bytes 12292
  437.4 6.6 %copy-start.58 = (f32[128,8]{1,0:T(8,128)S(1)}, f32[128,8]{1,0:T(8,128)}, u32[]{:S(2)}) copy-start(f32[128,8]{1,0:T(8,128)} %get-tuple-element.39) | copy-start | bytes 12292
  437.4 8.6 %copy-start.33 = (bf16[128,3072]{0,1:T(8,128)(2,1)S(1)}, bf16[128,3072]{0,1:T(8,128)(2,1)}, u32[]{:S(2)}) copy-start(bf16[128,3072]{0,1:T(8,128)(2,1)} %copy-done.32) | copy-start | bytes 2359300
  444.1 12.9 %slice-start = ((s8[12582912]{0:T(1024)(128)(4,1)}), s8[4194304]{0:T(1024)(128)(4,1)S(1)}, s32[]{:S(2)}) async-start(s8[12582912]{0:T(1024)(128)(4,1)} %bitcast.74), calls=%async_computation.3 | async-start | bytes 8388608
  446.0 5.2 copy-start.16
  446.0 11.0 %slice-start.1 = ((s8[12582912]{0:T(1024)(128)(4,1)}), s8[4194304]{0:T(1024)(128)(4,1)S(1)}, s32[]{:S(2)}) async-start(s8[12582912]{0:T(1024)(128)(4,1)} %bitcast.74), calls=%async_computation.4 | async-start | bytes 8388608
  451.2 4.6 copy-start.12
  572.0 4.6 copy-start.7
  (43 other events, 99.8 us)
Sparse Core Ops, SparseCore 0:
  21.1 113.4 all-gather.2
  245.3 184.8 all-reduce.4
  435.2 136.8 all-reduce.6

commit v2 on v1

v2 whole, which is shorter than its diff:
```python
import math, functools
import jax, jax.numpy as jnp
from jax import lax
from jax.sharding import PartitionSpec as P
from jax.experimental import pallas as pl
from jax.experimental.pallas import tpu as pltpu
D=1024
FF=4096
HEAD_DIM=128
SEG=512
MEM=384
COMP=512
RATE=3
KTOT=1408
RELN=1536
QB=128
EPSILON=1e-05
SCALE=1.0/math.sqrt(HEAD_DIM); NEG=-1e30
def tdot(a,b):
    return lax.dot_general(a,b,(((1,),(1,)),((),())),preferred_element_type=jnp.float32)
def ndot(a,b):
    return lax.dot_general(a,b,(((1,),(0,)),((),())),preferred_element_type=jnp.float32)
def cdot(a,b):
    return lax.dot_general(a,b,(((0,),(0,)),((),())),preferred_element_type=jnp.float32)

def attn_fwd_kernel(cnt_ref, qu_ref, qv_ref, k_ref, v_ref, r_ref, att_ref, p_ref):
    mc = cnt_ref[0]; cc = cnt_ref[1]
    kp = lax.broadcasted_iota(jnp.int32,(1,COMP+MEM),1)
    ok = ((kp < COMP) & (kp >= COMP-cc)) | ((kp>=COMP)&(kp>=COMP+MEM-mc))
    old_bias = jnp.where(ok, 0.0, NEG)
    tri = jnp.where(lax.broadcasted_iota(jnp.int32,(QB,QB),1) <= lax.broadcasted_iota(jnp.int32,(QB,QB),0), 0.0, NEG)
    for b in range(SEG//QB):
        i0=QB*b; nk=COMP+MEM+QB*(b+1); c0=SEG-QB-QB*b; wl=nk+QB
        s = tdot(qu_ref[pl.ds(i0,QB),:], k_ref[pl.ds(0,nk),:])
        w = tdot(qv_ref[pl.ds(i0,QB),:], r_ref[pl.ds(c0,wl),:])
        w = pltpu.roll(w, wl-(QB-1), 1, stride=1, stride_axis=0)[:,:nk]
        s = (s+w)*SCALE
        parts=[s[:,:COMP+MEM]+old_bias]
        if b: parts.append(s[:,COMP+MEM:nk-QB])
        parts.append(s[:,nk-QB:]+tri)
        s=jnp.concatenate(parts,axis=1)
        m=jnp.max(s,axis=1,keepdims=True)
        e=jnp.exp(s-m)
        l=jnp.sum(e,axis=1,keepdims=True)
        p=(e*(1.0/l)).astype(jnp.bfloat16)
        p_ref[0,pl.ds(i0,QB),pl.ds(0,nk)]=p
        if nk<KTOT: p_ref[0,pl.ds(i0,QB),pl.ds(nk,KTOT-nk)]=jnp.zeros((QB,KTOT-nk),jnp.bfloat16)
        att_ref[pl.ds(i0,QB),:]=ndot(p,v_ref[pl.ds(0,nk),:]).astype(jnp.bfloat16)

def attn_fwd(cnt,qu,qv,k,v,r):
    nh=qu.shape[1]//HEAD_DIM
    col=lambda n: pl.BlockSpec((n,HEAD_DIM),lambda h:(0,h))
    return pl.pallas_call(attn_fwd_kernel, grid=(nh,),
        in_specs=[pl.BlockSpec(memory_space=pltpu.SMEM),col(SEG),col(SEG),col(KTOT),col(KTOT),col(RELN)],
        out_specs=[col(SEG),pl.BlockSpec((1,SEG,KTOT),lambda h:(h,0,0))],
        out_shape=[jax.ShapeDtypeStruct((SEG,nh*HEAD_DIM),jnp.bfloat16),jax.ShapeDtypeStruct((nh,SEG,KTOT),jnp.bfloat16)],
        compiler_params=pltpu.CompilerParams(vmem_limit_bytes=60<<20),
        cost_estimate=pl.CostEstimate(flops=6*nh*SEG*KTOT*HEAD_DIM,bytes_accessed=12<<20,transcendentals=nh*SEG*KTOT),
        name="attention_forward")(cnt,qu,qv,k,v,r)

def attn_bwd_kernel(p_ref, ga_ref, qu_ref, qv_ref, k_ref, v_ref, r_ref, dq_ref, du_ref, dv_ref, dk_ref, dval_ref, dr_ref, ds_s, dw_s, qvr_s):
    flip=((lax.broadcasted_iota(jnp.int32,(QB,QB),0)+lax.broadcasted_iota(jnp.int32,(QB,QB),1))==QB-1).astype(jnp.float32).astype(jnp.bfloat16)
    du=jnp.zeros((1,HEAD_DIM),jnp.float32); dv=du
    for b in range(SEG//QB):
        i0=QB*b; nk=COMP+MEM+QB*(b+1); c0=SEG-QB-QB*b; wl=nk+QB
        rows=pl.ds(i0,QB)
        p=p_ref[0,rows,pl.ds(0,nk)].astype(jnp.float32)
        dp=tdot(ga_ref[rows,:],v_ref[pl.ds(0,nk),:])
        pd=p*dp
        delta=jnp.sum(pd,axis=1,keepdims=True)
        ds=(pd-p*delta).astype(jnp.bfloat16)
        ds_s[rows,pl.ds(0,nk)]=ds
        if nk<KTOT: ds_s[rows,pl.ds(nk,KTOT-nk)]=jnp.zeros((QB,KTOT-nk),jnp.bfloat16)
        wide=jnp.concatenate([ndot(flip,ds),jnp.zeros((QB,QB),jnp.float32)],axis=1)
        wide=pltpu.roll(wide,0,1,stride=1,stride_axis=0).astype(jnp.bfloat16)
        qvr_s[rows,:]=ndot(flip,qv_ref[rows,:]).astype(jnp.bfloat16)
        dw_s[rows,pl.ds(c0,wl)]=wide
        if c0: dw_s[rows,pl.ds(0,c0)]=jnp.zeros((QB,c0),jnp.bfloat16)
        dqu=ndot(ds,k_ref[pl.ds(0,nk),:])*SCALE
        dqr=ndot(wide,r_ref[pl.ds(c0,wl),:])*SCALE
        hi=dqr.astype(jnp.bfloat16); lo=(dqr-hi.astype(jnp.float32)).astype(jnp.bfloat16)
        dqv=ndot(flip,hi)+ndot(flip,lo)
        du+=jnp.sum(dqu,axis=0,keepdims=True); dv+=jnp.sum(dqv,axis=0,keepdims=True)
        dq_ref[rows,:]=(dqu+dqv).astype(jnp.bfloat16)
    du_ref[...]=du; dv_ref[...]=dv
    dk_ref[...]=(cdot(ds_s[...],qu_ref[...])*SCALE).astype(jnp.bfloat16)
    dr_ref[...]=(cdot(dw_s[...],qvr_s[...])*SCALE).astype(jnp.bfloat16)
    dval_ref[...]=cdot(p_ref[0],ga_ref[...]).astype(jnp.bfloat16)

def attn_bwd(p,ga,qu,qv,k,v,r):
    nh=qu.shape[1]//HEAD_DIM
    col=lambda n: pl.BlockSpec((n,HEAD_DIM),lambda h:(0,h))
    sd=lambda n,dt=jnp.bfloat16: jax.ShapeDtypeStruct((n,nh*HEAD_DIM),dt)
    return pl.pallas_call(attn_bwd_kernel, grid=(nh,),
        in_specs=[pl.BlockSpec((1,SEG,KTOT),lambda h:(h,0,0)),col(SEG),col(SEG),col(SEG),col(KTOT),col(KTOT),col(RELN)],
        out_specs=[col(SEG),col(1),col(1),col(KTOT),col(KTOT),col(RELN)],
        out_shape=[sd(SEG),sd(1,jnp.float32),sd(1,jnp.float32),sd(KTOT),sd(KTOT),sd(RELN)],
        scratch_shapes=[pltpu.VMEM((SEG,KTOT),jnp.bfloat16),pltpu.VMEM((SEG,RELN),jnp.bfloat16),pltpu.VMEM((SEG,HEAD_DIM),jnp.bfloat16)],
        compiler_params=pltpu.CompilerParams(vmem_limit_bytes=60<<20),
        cost_estimate=pl.CostEstimate(flops=12*nh*SEG*KTOT*HEAD_DIM,bytes_accessed=20<<20,transcendentals=0),
        name="attention_backward")(p,ga,qu,qv,k,v,r)


PATHS = {"A": ("x", "z", "y"), "B": ("y", "x", "z"), "C": ("z", "y", "x")}
SPOT = {"A": (0, 0, 0), "B": (0, 1, 1), "C": (0, 0, 2)}
STRIDE = {"y": 16, "z": 4, "x": 1}
ALL_AXES = ("dp", "blk")
BUFFER = 5648
ANY = pl.BlockSpec(memory_space=pl.ANY)
SMEM = pl.BlockSpec(memory_space=pltpu.SMEM)
VMEM = pl.BlockSpec(memory_space=pltpu.VMEM)
HBM = pl.BlockSpec(memory_space=pltpu.HBM)


def params(mib=40):
    return pltpu.CompilerParams(vmem_limit_bytes=mib << 20)


def shape_of(shape, dtype=jnp.float32):
    return jax.ShapeDtypeStruct(shape, dtype)


def swap(array):
    return lax.ppermute(array, "blk", [(0, 1), (1, 0)])


def step_pairs(chain, phase, delta):
    pairs = []
    for chip in range(64):
        for core in range(2):
            stride = STRIDE[PATHS[chain[core]][phase]]
            at = (chip // stride) % 4
            pairs.append((2 * chip + core, 2 * (chip + ((at + delta) % 4 - at) * stride) + core))
    return pairs


def send(array, chain, phase, delta):
    return lax.ppermute(array, ALL_AXES, step_pairs(chain, phase, delta))


def run_copies(copies):
    for copy in copies:
        copy.start()
    for copy in copies:
        copy.wait()


def spot_of(chain, core, phase, index):
    return (slice(None),) * SPOT[chain[core]][phase] + (index,)


def place_kernel(chain, phase, moves, deps, at_ref, own_ref, next_ref, across_ref, prev_ref, *rest):
    outs, sems = rest[deps:-1], rest[-1]
    pieces = (own_ref, next_ref, across_ref, prev_ref)
    lead = (slice(None),) * phase
    for core in range(2):
        @pl.when(at_ref[4] == core)
        def _():
            copies = []
            for k, piece in enumerate(pieces):
                where = spot_of(chain, core, phase, at_ref[k])
                for n, (start, size, out, head, to) in enumerate(moves):
                    source = piece.at[lead + (pl.ds(start, size),)]
                    target = outs[out].at[head + where]
                    if to is not None:
                        target = target.at[lead + (pl.ds(to, size),)]
                    copies.append(pltpu.make_async_copy(source, target, sems.at[k * len(moves) + n]))
            run_copies(copies)


def place(chain, phase, at, pieces, shapes, moves, deps=()):
    out = pl.pallas_call(
        functools.partial(place_kernel, chain, phase, moves, len(deps)),
        in_specs=[SMEM] + [ANY] * (4 + len(deps)),
        out_specs=[VMEM] * len(shapes),
        out_shape=[shape_of(shape, jnp.bfloat16) for shape in shapes],
        scratch_shapes=[pltpu.SemaphoreType.DMA((4 * len(moves),))],
        compiler_params=params(32),
        name="place_pieces",
    )(at, *pieces, *deps)
    return out if len(shapes) > 1 else out[0]


def grow(chain, phase, at, pieces):
    rows, lanes = pieces[0].shape[-2:]
    return place(chain, phase, at, pieces, [(4,) * (phase + 1) + (rows, lanes)], ((0, rows, 0, (), None),))


def send_pieces(chain, phase, at_ref, held, pieces, sems):
    for core in range(2):
        @pl.when(at_ref[4] == core)
        def _():
            copies = []
            for k, piece in enumerate(pieces):
                where = spot_of(chain, core, phase, at_ref[k])
                copies.append(pltpu.make_async_copy(held.at[where], piece, sems.at[k]))
            run_copies(copies)


def split_kernel(chain, phase, at_ref, own_in, one_in, two_in, three_in, own_ref, next_ref, across_ref, prev_ref, held, sems):
    held[...] = sum(ref[...].astype(jnp.float32) for ref in (own_in, one_in, two_in, three_in)).astype(jnp.bfloat16)
    send_pieces(chain, phase, at_ref, held, (own_ref, next_ref, across_ref, prev_ref), sems)


def add_split(chain, phase, at, parts):
    shape = parts[0].shape
    return pl.pallas_call(
        functools.partial(split_kernel, chain, phase),
        in_specs=[SMEM] + [VMEM] * 4,
        out_specs=[ANY] * 4,
        out_shape=[shape_of(shape[1:], jnp.bfloat16)] * 4,
        scratch_shapes=[pltpu.VMEM(shape, jnp.bfloat16), pltpu.SemaphoreType.DMA((4,))],
        compiler_params=params(32),
        name="add_pieces",
    )(at, *parts)


def finish_kernel(chain, at_ref, own_ref, next_ref, across_ref, prev_ref, *rest):
    outs, proj_ref, extra_ref, held, sems = rest[:4], rest[4], rest[5], rest[6], rest[7]
    for core in range(2):
        @pl.when(at_ref[4] == core)
        def _():
            copies = []
            for k, piece in enumerate((own_ref, next_ref, across_ref, prev_ref)):
                where = spot_of(chain, core, 2, at_ref[k])
                copies.append(pltpu.make_async_copy(piece, held.at[where], sems.at[k]))
            run_copies(copies)
    extra_ref[...] = held[0, 0, 0, 80:, :].astype(jnp.float32)
    for chip in range(64):
        y, z, x = chip // 16, (chip // 4) % 4, chip % 4
        for h in range(2):
            block = held[y, z, x, 32 * h : 32 * h + 32, :].astype(jnp.float32)
            outs[y][pl.ds(32 * (chip % 16), 32), pl.ds(512 * h, 512)] = block
            block = held[y, z, x, 64 + 8 * h : 72 + 8 * h, :].astype(jnp.float32)
            proj_ref[pl.ds(8 * chip, 8), pl.ds(512 * h, 512)] = block


def finish(chain, at, pieces):
    return pl.pallas_call(
        functools.partial(finish_kernel, chain),
        in_specs=[SMEM] + [ANY] * 4,
        out_specs=[VMEM] * 6,
        out_shape=[shape_of((512, D))] * 5 + [shape_of((8, 512))],
        scratch_shapes=[pltpu.VMEM((4, 4, 4, 88, 512), jnp.bfloat16), pltpu.SemaphoreType.DMA((4,))],
        compiler_params=params(60),
        name="finish_gradients",
    )(at, *pieces)


def three_ways(chain, phase, chunk):
    prev, nxt, across = send(chunk, chain, phase, 1), send(chunk, chain, phase, -1), send(chunk, chain, phase, 2)
    return chunk, nxt, across, prev


MATS = (4, 4, 4, 4, 16, 512)


def gather_steps(chain, chunk, spots, deps):
    chunk = grow(chain, 0, spots[0], three_ways(chain, 0, chunk))
    pieces = three_ways(chain, 1, chunk)
    near = place(chain, 1, spots[1], pieces, [(4, 4, 72, 512)], ((0, 64, 0, (), 0), (128, 8, 0, (), 64)))
    each = tuple((16 * m, 16, 0, (m,), None) for m in range(4))
    mats, vecs = place(
        chain, 2, spots[2], three_ways(chain, 2, near), [MATS, (4, 4, 4, 8, 512)], each + ((64, 8, 1, (), None),), deps
    )
    far = place(chain, 1, spots[1], pieces, [(4, 4, 64, 512)], ((64, 64, 0, (), None),), (mats,))
    panels = place(chain, 2, spots[2], three_ways(chain, 2, far), [MATS], each)
    return mats.reshape(4, D, 512), vecs, panels.reshape(4, D, 512)


def scatter_steps(chain, pieces, spots):
    for phase in (2, 1, 0):
        own, nxt, across, prev = pieces
        parts = (own, send(nxt, chain, phase, 1), send(prev, chain, phase, -1), send(across, chain, phase, 2))
        if phase:
            pieces = add_split(chain, phase - 1, spots[phase - 1], parts)
    return sum(part.astype(jnp.float32) for part in parts)


def regather_steps(chain, chunk, spots):
    for phase in range(2):
        chunk = grow(chain, phase, spots[phase], three_ways(chain, phase, chunk))
    return finish(chain, spots[2], three_ways(chain, 2, chunk))


PACKED = ((8, D),) * 4 + ((8, FF), (8, D), (24, D), (32, D)) + ((1, 8),) * 4 + ((1, 32), (1, 8), (1, 8))


def pack_kernel(at_ref, *refs):
    f32, bf16 = jnp.float32, jnp.bfloat16
    count = len(PACKED)
    sources, (blocks_ref, keep_ref, give_ref), held, sems = refs[:count], refs[count : count + 3], refs[count + 3 : -1], refs[-1]
    run_copies([pltpu.make_async_copy(source, place, sems.at[k]) for k, (source, place) in enumerate(zip(sources, held))])
    wq, wk, wv, wr, win, wp, wc, wo, ga, ub, vb, gf, bi, bo, bc = held
    first = at_ref[0] == 0
    where = at_ref[1]

    def spread(ref, size, width):
        row = lax.broadcasted_iota(jnp.int32, (size, width), 0)
        lane = lax.broadcasted_iota(jnp.int32, (size, width), 1)
        hot = (lane == size * where + row).astype(f32).astype(bf16)
        return ndot(ref[...], hot)

    for n, ref in enumerate((wq, wk, wv, wr)):
        left, right = ref[:, :512].astype(f32), ref[:, 512:].astype(f32)
        keep_ref[8 * n : 8 * n + 8, :] = jnp.where(first, left, right).astype(bf16)
        give_ref[8 * n : 8 * n + 8, :] = jnp.where(first, right, left).astype(bf16)
    for n in range(4):
        left, right = (win[:, 2048 * h + 512 * n : 2048 * h + 512 * n + 512].astype(f32) for h in range(2))
        keep_ref[32 + 8 * n : 40 + 8 * n, :] = jnp.where(first, left, right).astype(bf16)
        give_ref[32 + 8 * n : 40 + 8 * n, :] = jnp.where(first, right, left).astype(bf16)
    rows = []
    for ref in (ga, ub, vb, gf):
        wide = spread(ref, 8, D)
        rows += [wide[:, :512], wide[:, 512:]]
    vectors = jnp.concatenate(rows, axis=0).astype(bf16)
    keep_ref[64:72, :] = vectors
    give_ref[64:72, :] = vectors
    blocks_ref[0] = wp[...]
    for q in range(3):
        blocks_ref[1 + q] = wc[8 * q : 8 * q + 8, :]
    for q in range(4):
        blocks_ref[4 + q] = wo[8 * q : 8 * q + 8, :]
    wide = spread(bi, 32, 4 * D)
    rows = [wide[:, D * c : D * c + D] for c in range(4)] + [spread(bo, 8, D), spread(bc, 8, D), jnp.zeros((2, D), f32)]
    blocks_ref[8] = jnp.concatenate(rows, axis=0).astype(bf16)


def pack(at, *arrays):
    return pl.pallas_call(
        pack_kernel,
        in_specs=[SMEM] + [HBM] * len(arrays),
        out_specs=[VMEM] * 3,
        out_shape=[shape_of((9, 8, D), jnp.bfloat16)] + [shape_of((72, 512), jnp.bfloat16)] * 2,
        scratch_shapes=[pltpu.VMEM(shape, jnp.bfloat16) for shape in PACKED] + [pltpu.SemaphoreType.DMA((len(PACKED),))],
        compiler_params=params(60),
        name="pack_weights",
    )(at, *arrays)


def start_kernel(taps_ref, grad_ref, out_ref, stage, sem):
    stage[...] = cdot(taps_ref[...], grad_ref[...]).astype(jnp.bfloat16)
    run_copies([pltpu.make_async_copy(stage, out_ref.at[pl.ds(4096, 1536)], sem)])


def start_buffer(taps, grads):
    return pl.pallas_call(
        start_kernel,
        in_specs=[VMEM, VMEM],
        out_specs=HBM,
        out_shape=shape_of((BUFFER, D), jnp.bfloat16),
        scratch_shapes=[pltpu.VMEM((1536, D), jnp.bfloat16), pltpu.SemaphoreType.DMA],
        compiler_params=params(60),
        name="compression_gradient",
    )(taps, grads)


def normalize(rows):
    centred = rows - jnp.mean(rows, axis=1, keepdims=True)
    inverse = lax.rsqrt(jnp.mean(centred * centred, axis=1, keepdims=True) + EPSILON)
    return centred * inverse, inverse


def mix_kernel(core_ref, att_ref, got_ref, proj_ref, seg_ref, gain_ref, hidden_ref, act_ref):
    core = core_ref[0]
    mine = proj_ref[0, pl.ds(pl.multiple_of(512 * core, 512), 512), :]
    other = proj_ref[0, pl.ds(pl.multiple_of(512 - 512 * core, 512), 512), :]
    hidden = seg_ref[...].astype(jnp.float32) + ndot(att_ref[...], mine) + ndot(got_ref[...], other)
    hidden_ref[...] = hidden
    act_ref[...] = (normalize(hidden)[0] * gain_ref[...]).astype(jnp.bfloat16)


def mix(core, att, got, large, seg, gain):
    whole = lambda *shape: pl.BlockSpec(shape, lambda i: (0,) * len(shape))
    return pl.pallas_call(
        mix_kernel,
        grid=(1,),
        in_specs=[SMEM, whole(512, 512), whole(512, 512), whole(1, D, D), whole(512, D), whole(1, D)],
        out_specs=[whole(512, D), whole(512, D)],
        out_shape=[shape_of((512, D)), shape_of((512, D), jnp.bfloat16)],
        compiler_params=params(60),
        name="hidden_rows",
    )(core, att, got, large, seg, gain)


def middle_kernel(core_ref, back_ref, got_ref, hidden_ref, gain_ref, gr_ref, proj_ref, hid_ref, branch_ref, att_ref, sum_ref):
    del core_ref
    back = back_ref[...] + got_ref[...]
    normed, inverse = normalize(hidden_ref[...])
    sum_ref[...] = jnp.sum(back * normed, axis=0, keepdims=True)
    scaled = back * gain_ref[...]
    along = jnp.mean(scaled * normed, axis=1, keepdims=True)
    grad = gr_ref[...].astype(jnp.float32) + inverse * (
        scaled - jnp.mean(scaled, axis=1, keepdims=True) - normed * along
    )
    hid_ref[...] = grad
    branch = grad.astype(jnp.bfloat16)
    branch_ref[...] = branch
    att_ref[...] = tdot(branch, proj_ref[0]).astype(jnp.bfloat16)


def middle(core, back, got, hidden, gain, grad_res, large):
    whole = lambda *shape: pl.BlockSpec(shape, lambda i, c: (0,) * len(shape))
    return pl.pallas_call(
        middle_kernel,
        grid_spec=pltpu.PrefetchScalarGridSpec(
            num_scalar_prefetch=1,
            grid=(1,),
            in_specs=[
                whole(512, D), whole(512, D), whole(512, D), whole(1, D), whole(512, D),
                pl.BlockSpec((1, 512, D), lambda i, c: (0, c[0], 0)),
            ],
            out_specs=[whole(512, D), whole(512, D), whole(512, 512), whole(1, D)],
        ),
        out_shape=[
            shape_of((512, D)), shape_of((512, D), jnp.bfloat16), shape_of((512, 512), jnp.bfloat16), shape_of((1, D)),
        ],
        compiler_params=params(60),
        name="hidden_gradient",
    )(core, back, got, hidden, gain, grad_res, large)


LATE = ((512, 512), (512, D), (KTOT, D), (512, 512), (3, D, 512), (KTOT, 512), (KTOT, 512), (RELN, D), (RELN, 512))


def late_kernel(at_ref, *refs):
    f32, bf16 = jnp.float32, jnp.bfloat16
    count = len(LATE)
    sources, (gain_ref, small_ref), pieces = refs[:count], refs[count : count + 2], refs[count + 2 : count + 6]
    places, held, sems = refs[count + 6 : -2], refs[-2], refs[-1]
    loads = []
    for k, (source, to) in enumerate(zip(sources, places)):
        source = source.at[pl.ds(0, 3)] if k == 4 else source
        loads.append(pltpu.make_async_copy(source, to, sems.at[4 + k]))
        loads[-1].start()
    att_ref, branch_ref, joined_ref, gq_ref, mats_ref, gk_ref, gv_ref, table_ref, gr_ref = places
    loads[0].wait()
    loads[1].wait()
    proj = cdot(att_ref[...], branch_ref[...]).astype(bf16).reshape(4, 4, 4, 8, D)
    for h in range(2):
        held[:, :, :, 64 + 8 * h : 72 + 8 * h, :] = proj[..., 512 * h : 512 * h + 512]
    ones = jnp.ones((8, 512), bf16)
    total = jnp.zeros((8, D), f32)
    sides = (
        (lambda: joined_ref[pl.ds(COMP + MEM, SEG), :], gq_ref, (2, 3, 4)),
        (lambda: joined_ref[...], gk_ref, (5,)),
        (lambda: joined_ref[...], gv_ref, (6,)),
        (lambda: table_ref[...], gr_ref, (7, 8)),
    )
    for m, (left, right, needs) in enumerate(sides):
        for k in needs:
            loads[k].wait()
        grad = cdot(left(), right[...])
        low = grad.astype(bf16)
        for h in range(2):
            held[m, :, :, 32 * h : 32 * h + 32, :] = low[512 * h : 512 * h + 512].reshape(4, 4, 32, 512)
        if m < 3:
            product = grad * mats_ref[m].astype(f32)
            high = product.astype(bf16)
            total += tdot(ones, high) + tdot(ones, (product - high.astype(f32)).astype(bf16))
    total = total[:1] / gain_ref[...]
    extra = jnp.concatenate([total[:, :512], total[:, 512:], small_ref[2:, :]], axis=0)
    held[:, :, :, 80:, :] = jnp.zeros((4, 4, 4, 8, 512), bf16)
    held[0, 0, 0, 80:, :] = extra.astype(bf16)
    send_pieces("AB", 2, at_ref, held, pieces, sems)


def late_gradients(*arrays):
    bf16 = jnp.bfloat16
    return pl.pallas_call(
        late_kernel,
        in_specs=[SMEM] + [HBM] * len(LATE) + [VMEM] * 2,
        out_specs=[ANY] * 4,
        out_shape=[shape_of((4, 4, 88, 512), bf16)] * 4,
        scratch_shapes=[pltpu.VMEM(shape, bf16) for shape in LATE]
        + [pltpu.VMEM((4, 4, 4, 88, 512), bf16), pltpu.SemaphoreType.DMA((4 + len(LATE),))],
        compiler_params=params(60),
        cost_estimate=pl.CostEstimate(flops=2 * 5400 * 512 * 1024, bytes_accessed=24 << 20, transcendentals=0),
        name="late_gradients",
    )(*arrays)


def ffn_kernel(core_ref, act_ref, gr_ref, win_ref, *rest):
    del core_ref
    quarters, bias_ref, out_ref, back_ref, part_ref = rest[:4], rest[4], rest[6], rest[7], rest[8]
    natural, stage_in, stage_out, sums, sems = rest[9:]
    p = pl.program_id(0)
    slot = lax.rem(p, 2)

    def sending(step, buffer):
        rows = pl.ds(pl.multiple_of(1024 * (step // 2), 1024), 1024)
        lanes = pl.ds(pl.multiple_of(512 * lax.rem(step, 2), 512), 512)
        below = pl.ds(pl.multiple_of(2048 + 512 * step, 512), 512)
        return [
            pltpu.make_async_copy(stage_in.at[buffer], out_ref.at[rows, lanes], sems.at[buffer]),
            pltpu.make_async_copy(stage_out.at[buffer], out_ref.at[below], sems.at[2 + buffer]),
        ]

    @pl.when(p >= 2)
    def _():
        for copy in sending(p - 2, slot):
            copy.wait()

    act, grad, w_one = act_ref[...], gr_ref[...], win_ref[0]
    for q in range(4):
        for shard in range(16):
            natural[32 * shard + 8 * q : 32 * shard + 8 * q + 8, :] = quarters[q][0, 8 * shard : 8 * shard + 8, :]
    w_two = natural[...]
    pre = ndot(act, w_one) + bias_ref[0]
    inner = math.sqrt(2.0 / math.pi)
    square = pre * pre
    tanh = jnp.tanh(inner * pre * (1.0 + 0.044715 * square))
    act_low = (0.5 * pre * (1.0 + tanh)).astype(jnp.bfloat16)
    slope = 0.5 * (1.0 + tanh) + (0.5 * inner) * pre * (1.0 - tanh * tanh) * (1.0 + (3.0 * 0.044715) * square)
    grad_act = tdot(grad, w_two)
    grad_pre = (grad_act * slope).astype(jnp.bfloat16)
    stage_in[slot] = cdot(act, grad_pre).astype(jnp.bfloat16)
    stage_out[slot] = cdot(act_low, grad).astype(jnp.bfloat16)
    for copy in sending(p, slot):
        copy.start()
    total = jnp.sum(grad_pre.astype(jnp.float32), axis=0, keepdims=True)
    total = jnp.concatenate([total, total], axis=1)
    row = lax.broadcasted_iota(jnp.int32, (16, D), 0)
    lane = lax.broadcasted_iota(jnp.int32, (16, D), 1)
    mine = (row == p // 2) & (lane // 512 == lax.rem(p, 2))

    @pl.when(p == 0)
    def _():
        sums[...] = jnp.zeros_like(sums)
        back_ref[...] = tdot(grad_pre, w_one)
        part_ref[...] = ndot(act_low, w_two)

    @pl.when(p > 0)
    def _():
        back_ref[...] += tdot(grad_pre, w_one)
        part_ref[...] += ndot(act_low, w_two)

    sums[...] = jnp.where(mine, total, sums[...].astype(jnp.float32)).astype(jnp.bfloat16)

    @pl.when(p == 3)
    def _():
        last = pltpu.make_async_copy(sums, out_ref.at[pl.ds(5632, 16)], sems.at[4])
        last.start()
        for copy in sending(p - 1, 1 - slot) + sending(p, slot):
            copy.wait()
        last.wait()


def ffn(core, act, grad, w_one, large, bias, buffer):
    f32, bf16 = jnp.float32, jnp.bfloat16
    whole = pl.BlockSpec((512, D), lambda p, c: (0, 0))
    quarter = lambda q: pl.BlockSpec((1, 128, D), lambda p, c: (4 + q, 4 * c[0] + p, 0))
    return pl.pallas_call(
        ffn_kernel,
        grid_spec=pltpu.PrefetchScalarGridSpec(
            num_scalar_prefetch=1,
            grid=(4,),
            in_specs=[
                whole,
                whole,
                pl.BlockSpec((1, D, 512), lambda p, c: (p, 0, 0)),
                *(quarter(q) for q in range(4)),
                pl.BlockSpec((1, 1, 512), lambda p, c: (p, 0, 0)),
                HBM,
            ],
            out_specs=[HBM, whole, whole],
            scratch_shapes=[
                pltpu.VMEM((512, D), bf16),
                pltpu.VMEM((2, D, 512), bf16),
                pltpu.VMEM((2, 512, D), bf16),
                pltpu.VMEM((16, D), bf16),
                pltpu.SemaphoreType.DMA((5,)),
            ],
        ),
        out_shape=[shape_of((BUFFER, D), bf16), shape_of((512, D)), shape_of((512, D))],
        input_output_aliases={9: 0},
        compiler_params=params(60),
        cost_estimate=pl.CostEstimate(flops=12 * 512 * 1024 * 2048, bytes_accessed=24 << 20, transcendentals=512 * 2048),
        name="feed_forward",
    )(core, act, grad, w_one, large, large, large, large, bias, buffer)


def hold_kernel(*refs):
    del refs


def hold(array, deps):
    return pl.pallas_call(
        hold_kernel,
        in_specs=[HBM] + [ANY] * len(deps),
        out_specs=HBM,
        out_shape=shape_of(array.shape, array.dtype),
        input_output_aliases={0: 0},
        compiler_params=params(60),
        name="after_others",
    )(array, *deps)


def pick_kernel(core_ref, source_ref, out_ref):
    del core_ref
    out_ref[...] = source_ref[...]


def pick_halves(core, buffer):
    return pl.pallas_call(
        pick_kernel,
        grid_spec=pltpu.PrefetchScalarGridSpec(
            num_scalar_prefetch=1,
            grid=(2,),
            in_specs=[pl.BlockSpec((512, D), lambda q, c: (2 * q + 1 - c[0], 0))],
            out_specs=pl.BlockSpec((512, D), lambda q, c: (q, 0)),
        ),
        out_shape=shape_of((D, D), jnp.bfloat16),
        compiler_params=params(60),
        name="other_half",
    )(core, buffer)


def on_device(
    segment, memory, compressed, mem_count, comp_count, attn_gain, w_query, w_key, w_value, u_bias, v_bias,
    w_rel, w_proj, ffn_gain, w_in, b_in, w_out, b_out, w_comp, b_comp, out_grad, comp_grad,
):
    f32, bf16 = jnp.float32, jnp.bfloat16
    core, chip = lax.axis_index("blk"), lax.axis_index("dp")
    first = core == 0
    core_at = core.reshape(1).astype(jnp.int32)
    coords = {"y": chip // 16, "z": (chip // 4) % 4, "x": chip % 4}
    spots = {}
    for chain in ("AB",):
        spots[chain] = []
        for phase in range(3):
            at = jnp.where(first, coords[PATHS[chain[0]][phase]], coords[PATHS[chain[1]][phase]])
            spots[chain].append(jnp.stack([(at + k) % 4 for k in range(4)] + [core]).astype(jnp.int32))

    def both(own, other, axis=0):
        return jnp.where(first, jnp.concatenate([own, other], axis), jnp.concatenate([other, own], axis))

    def half(array, which, axis):
        size = array.shape[axis] // 2
        return lax.dynamic_slice_in_dim(array, which * size, size, axis)

    where_at = jnp.stack([core, 2 * chip + core]).astype(jnp.int32)
    row = lambda vector: vector.reshape(1, -1)
    blocks, keep, give = pack(
        where_at, w_query, w_key, w_value, w_rel, w_in, w_proj, w_comp, w_out,
        row(attn_gain), row(u_bias), row(v_bias), row(ffn_gain), row(b_in), row(b_out), row(b_comp),
    )
    large = lax.all_gather(blocks, ALL_AXES, axis=1, tiled=True)
    got = swap(give)
    chunk = jnp.concatenate(
        [both(keep[8 * n : 8 * n + 8], got[8 * n : 8 * n + 8]) for n in range(8)] + [keep[64:] + got[64:]]
    )

    pieces = [both(array[0], swap(array[0])) for array in (compressed, memory, segment, out_grad, comp_grad)]
    seg_at = COMP + MEM
    grad_res, comp_flat = pieces[3], pieces[4]
    all_rows = jnp.concatenate(pieces[:3])

    def centre(rows):
        mean = jnp.mean(rows, axis=-1, keepdims=True)
        centred = rows - mean
        return mean, lax.rsqrt(jnp.mean(centred * centred, axis=-1, keepdims=True) + EPSILON)

    mean_one, inverse_one = centre(all_rows.astype(f32))

    distance = (KTOT - 1) - jnp.arange(RELN, dtype=f32)
    frequency = jnp.exp(jnp.arange(D // 2, dtype=f32) * (-2.0 * math.log(10000.0) / D))
    coarse = distance[::32, None] * frequency[None, :]
    fine = jnp.arange(32, dtype=f32)[:, None] * frequency[None, :]
    sin_a, cos_a = (trig(coarse)[:, None, :] for trig in (jnp.sin, jnp.cos))
    sin_b, cos_b = (trig(fine)[None, :, :] for trig in (jnp.sin, jnp.cos))
    sines, cosines = sin_a * cos_b - cos_a * sin_b, cos_a * cos_b + sin_a * sin_b
    table = jnp.concatenate([sines.reshape(RELN, 512), cosines.reshape(RELN, 512)], axis=1)
    table = jnp.where(distance[:, None] >= 0.0, table, 0.0).astype(bf16)

    slot = jnp.arange(MEM, dtype=jnp.int32)
    masked = jnp.where((slot >= MEM - mem_count[0])[:, None], pieces[1], jnp.zeros_like(pieces[1]))
    windows = masked.reshape(MEM // RATE, RATE * D)
    buffer = start_buffer(half(windows, core, 1), comp_flat)

    mats, vecs, w_one = gather_steps("AB", chunk, spots["AB"], (mean_one, inverse_one, all_rows, table, buffer))
    vecs = jnp.sum(vecs.astype(f32), axis=(0, 1, 2))
    gain_one, gain_two = vecs[:2].reshape(1, D), vecs[6:8].reshape(1, D)
    bias_u = jnp.where(first, vecs[2], vecs[3])
    bias_v = jnp.where(first, vecs[4], vecs[5])
    joined = ((all_rows.astype(f32) - mean_one) * inverse_one * gain_one).astype(bf16)
    query_rows = ndot(joined[seg_at:], mats[0])
    key_rows = ndot(joined, mats[1]).astype(bf16)
    value_rows = ndot(joined, mats[2]).astype(bf16)
    rel_rows = ndot(table, mats[3]).astype(bf16)
    query_u = (query_rows + bias_u).astype(bf16)
    query_v = (query_rows + bias_v).astype(bf16)
    counts = jnp.concatenate([mem_count, comp_count])
    attended, probs = attn_fwd(counts, query_u, query_v, key_rows, value_rows, rel_rows)

    others = jnp.sum(large[8].reshape(128, 8, D).astype(f32), axis=0)
    ffn_bias = half(others[:4], core, 0).reshape(4, 1, 512)
    out_bias, comp_bias = others[4], others[5]
    hidden, act_two = mix(core_at, attended, swap(attended), large, pieces[2], gain_two)
    buffer, back, partial = ffn(core_at, act_two, grad_res, w_one, large, ffn_bias, buffer)
    buffer = lax.psum(buffer, "dp")
    grad_hidden, grad_branch, grad_att, d_gain_two = middle(
        core_at, back, swap(back), hidden, gain_two, grad_res, large
    )

    grad_query, d_u, d_v, grad_keys, grad_values, grad_rel = attn_bwd(
        probs, grad_att, query_u, query_v, key_rows, value_rows, rel_rows
    )
    d_b_out = jnp.sum(half(grad_res, core, 1).astype(f32), axis=0, keepdims=True)
    d_b_comp = jnp.sum(half(comp_flat, core, 1).astype(f32), axis=0, keepdims=True)
    small = jnp.concatenate(
        [jnp.zeros((2, 512), f32), d_u, d_v, half(d_gain_two, core, 1), d_b_out, d_b_comp, jnp.zeros((1, 512), f32)]
    )
    pieces_late = late_gradients(
        spots["AB"][2], attended, grad_branch, joined, grad_query, mats, grad_keys, grad_values, table, grad_rel, gain_one, small
    )
    share = scatter_steps("AB", pieces_late, spots["AB"])
    keep = half(share[:64], core, 0).astype(bf16)
    mail = swap(jnp.concatenate([half(share[:64], 1 - core, 0), share[80:]]).astype(bf16))
    gains = jnp.where(jnp.arange(8)[:, None] < 2, share[80:] + mail[32:].astype(f32), share[80:])
    late = jnp.concatenate([both(keep, mail[:32]), share[64:80].astype(bf16), gains.astype(bf16)])
    *late, d_proj, extra = regather_steps("AB", late, spots["AB"])

    result = half(hidden, core, 0) + half(partial, core, 0) + swap(half(partial, 1 - core, 0)) + out_bias
    output = result.astype(bf16)

    comp_proj = large[1:4].reshape(3, 128, 8, D).transpose(1, 0, 2, 3).reshape(RATE * D, D)
    new_compressed = (ndot(half(windows, core, 0), comp_proj) + comp_bias).astype(bf16)

    grad_seg = (
        tdot(grad_query, mats[0]) + tdot(grad_keys[seg_at:], mats[1]) + tdot(grad_values[seg_at:], mats[2])
    )
    grad_seg = half(grad_seg, core, 0) + swap(half(grad_seg, 1 - core, 0))
    scaled_one = grad_seg * gain_one
    own_segment = segment[0].astype(f32)
    mean_seg, inverse_seg = centre(own_segment)
    normed_seg = (own_segment - mean_seg) * inverse_seg
    d_segment = half(grad_hidden, core, 0) + inverse_seg * (
        scaled_one
        - jnp.mean(scaled_one, axis=-1, keepdims=True)
        - normed_seg * jnp.mean(scaled_one * normed_seg, axis=-1, keepdims=True)
    )

    buffer = hold(buffer, (late[0], output, new_compressed, d_segment))
    others = swap(pick_halves(core_at, buffer))
    d_out = buffer[2048:4096].astype(f32)
    d_comp = buffer[4096:5632].astype(f32)
    mine = [lax.dynamic_slice_in_dim(buffer, D * q + 512 * core, 512, 0) for q in range(2)]
    d_in = both(jnp.concatenate(mine, axis=1), jnp.concatenate([others[:512], others[512:]], axis=1), 1).astype(f32)
    d_b_in = buffer[5632:5634].astype(f32).reshape(2048)
    return (
        output[None],
        new_compressed[None],
        d_segment[None],
        jnp.where(first, extra[0], extra[1]),
        late[0],
        late[1],
        late[2],
        extra[2],
        extra[3],
        late[3],
        d_proj,
        extra[4],
        d_in,
        d_b_in,
        d_out,
        extra[5],
        d_comp,
        extra[6],
    )


def solution(mesh):
    rows, weight, vector = P("dp", "blk", None), P(("dp", "blk"), None), P(("dp", "blk"))
    placed = (
        rows, rows, rows, P("dp"), P("dp"), vector, weight, weight, weight, vector, vector,
        weight, weight, vector, weight, vector, weight, vector, weight, vector, rows, rows,
    )
    half_one, half_two = P("blk"), P("blk", None)
    return jax.shard_map(
        on_device,
        mesh=mesh,
        in_specs=placed,
        out_specs=(
            rows, rows, rows, half_one, half_two, half_two, half_two, half_one, half_one,
            half_two, half_two, half_one, half_two, half_one, half_two, half_one, half_two, half_one,
        ),
        check_vma=False,
    )
```

time: 597 us -> 443 us (0.74)
  waiting for transfers between devices: 278 us -> 150 us
  local copies, waits for them, and re-layouts: 113 us -> 29.2 us
  Pallas kernels: 35.9 us -> 119 us
  matrix products: 72.1 us -> 16.4 us
  starting transfers between devices: 6.68 us -> 56.9 us
  other arithmetic: 66 us -> 46.3 us
    psum x2 -> x1, waiting for transfers between devices: 192 us -> 0.02 us  [on_device(): buffer = lax.psum(buffer, 'dp')]
    ppermute x0 -> x30, waiting for transfers between devices: none -> 147 us  [send(): return lax.ppermute(array, ALL_AXES, step_pairs(chain, phase, delta))]
    all_gather x1, waiting for transfers between devices: 85.9 us -> 0.01 us  [on_device(): large = lax.all_gather(blocks, ALL_AXES, axis=1, tiled=True)]
    pallas_call x0 -> x18, Pallas kernels: none -> 84 us  [the longest x1 21.2 us: ffn(): pl.pallas_call(ffn_kernel, grid_spec=pltpu.PrefetchScalarGridSpec(num_sca...]
    ppermute x0 -> x30, starting transfers between devices: none -> 40.1 us  [send(): return lax.ppermute(array, ALL_AXES, step_pairs(chain, phase, delta))]
    dot_general x13 -> x0, matrix products: 34.8 us -> none  [cdot(): lax.dot_general(a, b, (((0,), (0,)), ((), ())), preferred_element_type=jn...]
    slice x14 -> x11, local copies, waits for them, and re-layouts: 34.3 us -> 2 us  [the longest x1 0.86 us: on_device(): out_bias, comp_bias = (others[4], others[5])]
    unnamed x187 -> x73, local copies, waits for them, and re-layouts: 38.4 us -> 9.66 us
  transfers between devices with their start and end apart: 14 -> 44, of which waited for: 3 -> 17; matrix products, arithmetic and copies ran while one was open for 27% -> 18% of each run, Pallas kernels for 4% -> 20%
where the time goes in v2:
time: 443 us; the launch traced here: 435 us
  waiting for transfers between devices  150 us (34%)
  Pallas kernels  119 us (27%)
  starting transfers between devices  56.9 us (13%)
  other arithmetic  46.3 us (10%)
  local copies, waits for them, and re-layouts  29.2 us (7%)
  between operations  16.7 us (4%)
  matrix products  16.4 us (4%)
    ppermute x30, waiting for transfers between devices, send(): return lax.ppermute(array, ALL_AXES, step_pairs(chain, phase, delta))  147 us
    ppermute x30, starting transfers between devices, send(): return lax.ppermute(array, ALL_AXES, step_pairs(chain, phase, delta))  40.1 us
    pallas_call x1, Pallas kernels, ffn(): pl.pallas_call(ffn_kernel, grid_spec=pltpu.PrefetchScalarGridSpec(num_sca...  21.2 us
    pallas_call x1, Pallas kernels, attn_bwd(): pl.pallas_call(attn_bwd_kernel, grid=(nh,), in_specs=[pl.BlockSpec((1, SE...  21 us
    ppermute x12, starting transfers between devices, swap(): return lax.ppermute(array, 'blk', [(0, 1), (1, 0)])  16.7 us
    pallas_call x1, Pallas kernels, late_gradients(): pl.pallas_call(late_kernel, in_specs=[SMEM] + [HBM] * len(LATE) + [VMEM]...  14.9 us
    pallas_call x7, Pallas kernels, place(): pl.pallas_call(functools.partial(place_kernel, chain, phase, moves, len(d...  14.4 us
    pallas_call x1, Pallas kernels, attn_fwd(): pl.pallas_call(attn_fwd_kernel, grid=(nh,), in_specs=[pl.BlockSpec(memory...  13.9 us
  transfers between devices with their start and end apart: 44, of which 17 were waited for; matrix products, arithmetic and copies ran while one was open for 18% of the time, Pallas kernels for 20%

profile of v2, /device:TPU:1, one launch (start us, length us, event | category | flops | bytes accessed | tf_op | source)
XLA Modules:
  0.0 434.5 jit_solution(8709475212220678707)
XLA Ops:
  9.1 2.7 pack_weights.1
  18.7 2.6 collective-permute-start.5
  23.2 2.2 copy.42
  28.4 2.6 place_pieces.7.own_ref
  32.0 2.4 collective-permute-start.8
  35.6 2.5 maximum_select_fusion.5
  38.1 2.2 select_n.267
  43.3 3.7 compression_gradient.1.rest_4_.rest_5_
  47.1 2.5 collective-permute-start.15
  52.4 2.6 collective-permute-start.11
  61.6 11.4 %collective-permute-done.12.prev_ref = bf16[4,4,72,512]{3,2,1,0:T(8,128)(2,1)S(1)} collective-permute-done((bf16[4,4,72,512]{3,2,1,0:T(8,128)(2,1)S(1)}, bf16[4,4,72,512]{3,2,1,0:T(8,128)(2,1)S(1)}, u32[]{:S(2)}, u32[]{:S(2)}) %collective-permute-start.12) | collective-permute-done | bytes 1179680 | tf_op jit(solution)/shard_map/ppermute | solution.py:138
  73.0 12.8 %collective-permute-done.11.across_ref = bf16[4,4,72,512]{3,2,1,0:T(8,128)(2,1)S(1)} collective-permute-done((bf16[4,4,72,512]{3,2,1,0:T(8,128)(2,1)S(1)}, bf16[4,4,72,512]{3,2,1,0:T(8,128)(2,1)S(1)}, u32[]{:S(2)}, u32[]{:S(2)}) %collective-permute-start.11) | collective-permute-done | bytes 1179680 | tf_op jit(solution)/shard_map/ppermute | solution.py:138
  87.0 3.5 place_pieces.10.own_ref
  91.5 2.4 collective-permute-start.17
  96.4 2.8 convolution_convert_fusion.1.v_ref
  99.3 2.9 convolution_convert_fusion.r_ref
  102.2 2.8 convolution_convert_fusion.2.k_ref
  106.7 13.9 %attention_forward.1 = (bf16[512,512]{1,0:T(8,128)(2,1)}, bf16[4,512,1408]{2,1,0:T(8,128)(2,1)}) custom-call(s32[2]{0:T(128)} %get-tuple-element.150.cnt_ref, bf16[512,512]{1,0:T(8,128)(2,1)} %get-tuple-element.112.qu_ref, bf16[512,512]{1,0:T(8,128)(2,1)} %get-tuple-element.111.qv_ref, bf16[1408,512]{1,0:T(8,128)(2,1)} %convolution_convert_fusion.2.k_ref, ...), custom_call_target="tpu_custom_call" | custom-call | flops 2214592512 | bytes 12582912 | tf_op jit(solution)/shard_map/attention_forward/pallas_call | solution.py:53
  120.6 3.5 collective-permute-start.14
  124.1 3.1 maximum_select_fusion.4.gr_ref
  128.6 11.6 %collective-permute-done.17.across_ref = bf16[4,4,64,512]{3,2,1,0:T(8,128)(2,1)} collective-permute-done((bf16[4,4,64,512]{3,2,1,0:T(8,128)(2,1)}, bf16[4,4,64,512]{3,2,1,0:T(8,128)(2,1)}, u32[]{:S(2)}, u32[]{:S(2)}) %collective-permute-start.17) | collective-permute-done | bytes 1048608 | tf_op jit(solution)/shard_map/ppermute | solution.py:138
  140.2 3.3 place_pieces.11
  148.9 5.2 %hidden_rows.1 = (f32[512,1024]{1,0:T(8,128)}, bf16[512,1024]{1,0:T(8,128)(2,1)}) custom-call(s32[1]{0:T(128)} %bitcast.core_ref, bf16[512,512]{1,0:T(8,128)(2,1)} %get-tuple-element.62.att_ref.refs_0_, bf16[512,512]{1,0:T(8,128)(2,1)} %copy-done.30, bf16[9,1024,1024]{2,1,0:T(8,128)(2,1)} %all-gather.2.cloned.1.call-done.proj_ref.rest_0_.rest_1_.rest_2_.rest_3_, ...), custom_call_target="tpu_custom_call" | custom-call | tf_op jit(solution)/shard_map/hidden_rows/pallas_call | solution.py:375
  154.1 21.2 %feed_forward.1 = (bf16[5648,1024]{1,0:T(8,128)(2,1)}, f32[512,1024]{1,0:T(8,128)}, f32[512,1024]{1,0:T(8,128)}) custom-call(s32[1]{0:T(128)} %bitcast.core_ref, bf16[512,1024]{1,0:T(8,128)(2,1)} %get-tuple-element.65.act_ref, bf16[512,1024]{1,0:T(8,128)(2,1)} %maximum_select_fusion.4.gr_ref, ...), custom_call_target="tpu_custom_call", output_to_operand_aliasing={{0}: (9, {})} | custom-call | flops 12884901888 | bytes 25165824 | tf_op jit(solution)/shard_map/feed_forward/pallas_call | solution.py:553
  178.0 3.2 collective-permute-done.20.got_ref
  181.2 8.1 %hidden_gradient.1 = (f32[512,1024]{1,0:T(8,128)}, bf16[512,1024]{1,0:T(8,128)(2,1)}, bf16[512,512]{1,0:T(8,128)(2,1)}, f32[1,1024]{1,0:T(1,128)}) custom-call(s32[1]{0:T(128)} %bitcast.core_ref, f32[512,1024]{1,0:T(8,128)} %get-tuple-element.67.back_ref, f32[512,1024]{1,0:T(8,128)} %collective-permute-done.20.got_ref, ...), custom_call_target="tpu_custom_call" | custom-call | tf_op jit(solution)/shard_map/hidden_gradient/pallas_call | solution.py:404
  189.9 21.0 %attention_backward.1 = (bf16[512,512]{1,0:T(8,128)(2,1)}, f32[1,512]{1,0:T(1,128)}, f32[1,512]{1,0:T(1,128)}, bf16[1408,512]{1,0:T(8,128)(2,1)}, bf16[1408,512]{1,0:T(8,128)(2,1)}, /*index=5*/bf16[1536,512]{1,0:T(8,128)(2,1)}) custom-call(bf16[4,512,1408]{2,1,0:T(8,128)(2,1)} %get-tuple-element.69.p_ref, bf16[512,512]{1,0:T(8,128)(2,1)} %get-tuple-element.70.ga_ref, ...), custom_call_target="tpu_custom_call" | custom-call | flops 4429185024 | bytes 20971520 | tf_op jit(solution)/shard_map/attention_backward/pallas_call | solution.py:94
  212.3 14.9 %late_gradients.1 = (bf16[4,4,88,512]{3,2,1,0:T(8,128)(2,1)}, bf16[4,4,88,512]{3,2,1,0:T(8,128)(2,1)}, bf16[4,4,88,512]{3,2,1,0:T(8,128)(2,1)}, bf16[4,4,88,512]{3,2,1,0:T(8,128)(2,1)}) custom-call(s32[5]{0:T(128)} %copy-done.5, bf16[512,512]{1,0:T(8,128)(2,1)} %get-tuple-element.62.att_ref.refs_0_, bf16[512,1024]{1,0:T(8,128)(2,1)} %get-tuple-element.74.refs_1_, ...), custom_call_target="tpu_custom_call" | custom-call | flops 5662310400 | bytes 25165824 | tf_op jit(solution)/shard_map/late_gradients/pallas_call | solution.py:470
  227.3 2.7 collective-permute-start.23
  232.7 38.1 %collective-permute-done.22.one_in = bf16[4,4,88,512]{3,2,1,0:T(8,128)(2,1)S(1)} collective-permute-done((bf16[4,4,88,512]{3,2,1,0:T(8,128)(2,1)}, bf16[4,4,88,512]{3,2,1,0:T(8,128)(2,1)S(1)}, u32[]{:S(2)}, u32[]{:S(2)}) %collective-permute-start.22) | collective-permute-done | bytes 1441824 | tf_op jit(solution)/shard_map/ppermute | solution.py:138
  272.2 2.5 add_pieces.2
  283.7 4.1 collective-permute-done.27.three_in
  293.9 3.1 collective-permute-done.30
  297.1 2.4 collective-permute-start.31
  312.7 3.6 slice_bitcast_fusion
  317.9 3.9 collective-permute-done.37.prev_ref
  321.8 4.4 %collective-permute-done.36.across_ref = bf16[4,88,512]{2,1,0:T(8,128)(2,1)S(1)} collective-permute-done((bf16[4,88,512]{2,1,0:T(8,128)(2,1)S(1)}, bf16[4,88,512]{2,1,0:T(8,128)(2,1)S(1)}, u32[]{:S(2)}, u32[]{:S(2)}) %collective-permute-start.36) | collective-permute-done | bytes 360480 | tf_op jit(solution)/shard_map/ppermute | solution.py:138
  328.1 3.6 collective-permute-start.39
  334.3 2.7 add_convert_fusion.refs_2_
  340.1 20.0 %collective-permute-done.40.prev_ref = bf16[4,4,88,512]{3,2,1,0:T(8,128)(2,1)S(1)} collective-permute-done((bf16[4,4,88,512]{3,2,1,0:T(8,128)(2,1)S(1)}, bf16[4,4,88,512]{3,2,1,0:T(8,128)(2,1)S(1)}, u32[]{:S(2)}, u32[]{:S(2)}) %collective-permute-start.40) | collective-permute-done | bytes 1441824 | tf_op jit(solution)/shard_map/ppermute | solution.py:138
  360.1 31.4 %collective-permute-done.39.across_ref = bf16[4,4,88,512]{3,2,1,0:T(8,128)(2,1)S(1)} collective-permute-done((bf16[4,4,88,512]{3,2,1,0:T(8,128)(2,1)S(1)}, bf16[4,4,88,512]{3,2,1,0:T(8,128)(2,1)S(1)}, u32[]{:S(2)}, u32[]{:S(2)}) %collective-permute-start.39) | collective-permute-done | bytes 1441824 | tf_op jit(solution)/shard_map/ppermute | solution.py:138
  391.5 3.0 collective-permute-done.38.next_ref
  394.5 7.5 %finish_gradients.1 = (f32[512,1024]{1,0:T(8,128)}, f32[512,1024]{1,0:T(8,128)}, f32[512,1024]{1,0:T(8,128)}, f32[512,1024]{1,0:T(8,128)}, f32[512,1024]{1,0:T(8,128)}, /*index=5*/f32[8,512]{1,0:T(8,128)}) custom-call(s32[5]{0:T(128)} %copy-done.5, bf16[4,4,88,512]{3,2,1,0:T(8,128)(2,1)} %copy-done.3, ...), custom_call_target="tpu_custom_call" | custom-call | tf_op jit(solution)/shard_map/finish_gradients/pallas_call | solution.py:239
  402.0 2.6 other_half.1
  404.6 3.0 collective-permute-start.41
  411.3 5.3 %slice_convert_fusion.1 = f32[1536,1024]{1,0:T(8,128)} fusion(bf16[5648,1024]{1,0:T(8,128)(2,1)} %after_others.1.source_ref), kind=kLoop, calls=%fused_computation.14 | loop fusion | flops 1572864 | bytes 9437184 | tf_op jit(solution)/shard_map/convert_element_type | solution.py:747
  416.6 6.6 %slice_convert_fusion = f32[2048,1024]{1,0:T(8,128)} fusion(bf16[5648,1024]{1,0:T(8,128)(2,1)} %after_others.1.source_ref), kind=kLoop, calls=%fused_computation.10 | loop fusion | flops 2097152 | bytes 12582912 | tf_op jit(solution)/shard_map/convert_element_type | solution.py:746
  423.4 3.8 fusion.6
  (229 shorter events, 89.6 us)
Async XLA Ops:
  7.2 138.3 %all-gather.2.cloned.1.call-start = ((), (), s32[]{:S(2)}) async-start(), calls=%async_computation | async-start | bytes 19021824 | tf_op jit(solution)/shard_map/all_gather | solution.py:648
  11.8 390.1 %all-reduce.2.cloned.1.call-start = ((), (), s32[]{:S(2)}) async-start(), calls=%async_computation.1 | async-start | bytes 23134208 | tf_op jit(solution)/shard_map/psum | solution.py:701
  11.9 13.8 %collective-permute-start.13 = (bf16[64,1024]{1,0:T(8,128)(2,1)}, bf16[64,1024]{1,0:T(8,128)(2,1)}, u32[]{:S(2)}, u32[]{:S(2)}) collective-permute-start(bf16[64,1024]{1,0:T(8,128)(2,1)} %bitcast.115), channel_id=1, source_target_pairs={{0,1},{1,0},{2,3},{3,2},{4,5},{5,4},{6,7},{7,6},{8,9},{9,8},{10,11... | collective-permute-start | bytes 393224 | tf_op jit(solution)/shard_map/ppermute | solution.py:124
  13.4 3.7 collective-permute-start.3
  13.5 20.9 %collective-permute-start.1 = (bf16[192,1024]{1,0:T(8,128)(2,1)}, bf16[192,1024]{1,0:T(8,128)(2,1)}, u32[]{:S(2)}, u32[]{:S(2)}) collective-permute-start(bf16[192,1024]{1,0:T(8,128)(2,1)} %bitcast.113), channel_id=1, source_target_pairs={{0,1},{1,0},{2,3},{3,2},{4,5},{5,4},{6,7},{7,6},{8,9},{9,8},{10,11... | collective-permute-start | bytes 1179656 | tf_op jit(solution)/shard_map/ppermute | solution.py:124
  17.0 82.2 %copy-start.2 = (bf16[1536,1024]{1,0:T(8,128)(2,1)}, bf16[1536,1024]{1,0:T(8,128)(2,1)S(1)}, u32[]{:S(2)}) copy-start(bf16[1536,1024]{1,0:T(8,128)(2,1)S(1)} %fusion.2.rest_3_.refs_7_) | copy-start | bytes 9437188
  17.2 11.1 %collective-permute-start.6 = (bf16[136,512]{1,0:T(8,128)(2,1)S(1)}, bf16[136,512]{1,0:T(8,128)(2,1)S(1)}, u32[]{:S(2)}, u32[]{:S(2)}) collective-permute-start(bf16[136,512]{1,0:T(8,128)(2,1)S(1)} %constant_dynamic-update-slice_fusion.own_ref), channel_id=1, source_target_pairs={{0,2},{1,33},{2,4},{3,35},{4,6},{5,37},{6,0},{7,39},{8,10},{9,41},... | collective-permute-start | bytes 417800 | tf_op jit(solution)/shard_map/ppermute | solution.py:138
  18.7 9.7 %collective-permute-start.5 = (bf16[136,512]{1,0:T(8,128)(2,1)S(1)}, bf16[136,512]{1,0:T(8,128)(2,1)}, u32[]{:S(2)}, u32[]{:S(2)}) collective-permute-start(bf16[136,512]{1,0:T(8,128)(2,1)S(1)} %constant_dynamic-update-slice_fusion.own_ref), channel_id=1, source_target_pairs={{0,4},{1,65},{2,6},{3,67},{4,0},{5,69},{6,2},{7,71},{8,12},{9,73},... | collective-permute-start | bytes 417800 | tf_op jit(solution)/shard_map/ppermute | solution.py:138
  21.3 7.1 %collective-permute-start.4 = (bf16[136,512]{1,0:T(8,128)(2,1)S(1)}, bf16[136,512]{1,0:T(8,128)(2,1)}, u32[]{:S(2)}, u32[]{:S(2)}) collective-permute-start(bf16[136,512]{1,0:T(8,128)(2,1)S(1)} %constant_dynamic-update-slice_fusion.own_ref), channel_id=1, source_target_pairs={{0,6},{1,97},{2,0},{3,99},{4,2},{5,101},{6,4},{7,103},{8,14},{9,10... | collective-permute-start | bytes 417800 | tf_op jit(solution)/shard_map/ppermute | solution.py:138
  25.6 114.5 %copy-start.5 = (s32[5]{0:T(128)}, s32[5]{0:T(128)S(1)}, u32[]{:S(2)}) copy-start(s32[5]{0:T(128)S(1)} %stack.59.at_ref) | copy-start | bytes 64
  25.7 29.2 %collective-permute-start = (bf16[256,1024]{1,0:T(8,128)(2,1)}, bf16[256,1024]{1,0:T(8,128)(2,1)}, u32[]{:S(2)}, u32[]{:S(2)}) collective-permute-start(bf16[256,1024]{1,0:T(8,128)(2,1)} %bitcast.111), channel_id=1, source_target_pairs={{0,1},{1,0},{2,3},{3,2},{4,5},{5,4},{6,7},{7,6},{8,9},{9,8},{10,11... | collective-permute-start | bytes 1572872 | tf_op jit(solution)/shard_map/ppermute | solution.py:124
  28.4 29.2 %collective-permute-start.2 = (bf16[256,1024]{1,0:T(8,128)(2,1)}, bf16[256,1024]{1,0:T(8,128)(2,1)}, u32[]{:S(2)}, u32[]{:S(2)}) collective-permute-start(bf16[256,1024]{1,0:T(8,128)(2,1)} %bitcast.96), channel_id=1, source_target_pairs={{0,1},{1,0},{2,3},{3,2},{4,5},{5,4},{6,7},{7,6},{8,9},{9,8},{10,11... | collective-permute-start | bytes 1572872 | tf_op jit(solution)/shard_map/ppermute | solution.py:124
  31.0 16.1 %collective-permute-start.9 = (bf16[4,136,512]{2,1,0:T(8,128)(2,1)}, bf16[4,136,512]{2,1,0:T(8,128)(2,1)}, u32[]{:S(2)}, u32[]{:S(2)}) collective-permute-start(bf16[4,136,512]{2,1,0:T(8,128)(2,1)} %place_pieces.7.own_ref), channel_id=1, source_target_pairs={{0,8},{1,3},{2,10},{3,5},{4,12},{5,7},{6,14},{7,1},{8,16},{9,11},{... | collective-permute-start | bytes 1671176 | tf_op jit(solution)/shard_map/ppermute | solution.py:138
  32.0 17.7 %collective-permute-start.8 = (bf16[4,136,512]{2,1,0:T(8,128)(2,1)}, bf16[4,136,512]{2,1,0:T(8,128)(2,1)}, u32[]{:S(2)}, u32[]{:S(2)}) collective-permute-start(bf16[4,136,512]{2,1,0:T(8,128)(2,1)} %place_pieces.7.own_ref), channel_id=1, source_target_pairs={{0,16},{1,5},{2,18},{3,7},{4,20},{5,1},{6,22},{7,3},{8,24},{9,13},... | collective-permute-start | bytes 1671176 | tf_op jit(solution)/shard_map/ppermute | solution.py:138
  34.4 15.2 %collective-permute-start.7 = (bf16[4,136,512]{2,1,0:T(8,128)(2,1)}, bf16[4,136,512]{2,1,0:T(8,128)(2,1)}, u32[]{:S(2)}, u32[]{:S(2)}) collective-permute-start(bf16[4,136,512]{2,1,0:T(8,128)(2,1)} %place_pieces.7.own_ref), channel_id=1, source_target_pairs={{0,24},{1,7},{2,26},{3,1},{4,28},{5,3},{6,30},{7,5},{8,0},{9,15},{... | collective-permute-start | bytes 1671176 | tf_op jit(solution)/shard_map/ppermute | solution.py:138
  47.1 77.0 %collective-permute-start.15 = (bf16[256,1024]{1,0:T(8,128)(2,1)}, bf16[256,1024]{1,0:T(8,128)(2,1)}, u32[]{:S(2)}, u32[]{:S(2)}) collective-permute-start(bf16[256,1024]{1,0:T(8,128)(2,1)} %bitcast.35), channel_id=1, source_target_pairs={{0,1},{1,0},{2,3},{3,2},{4,5},{5,4},{6,7},{7,6},{8,9},{9,8},{10,11... | collective-permute-start | bytes 1572872 | tf_op jit(solution)/shard_map/ppermute | solution.py:124
  51.8 21.3 %collective-permute-start.12 = (bf16[4,4,72,512]{3,2,1,0:T(8,128)(2,1)S(1)}, bf16[4,4,72,512]{3,2,1,0:T(8,128)(2,1)S(1)}, u32[]{:S(2)}, u32[]{:S(2)}) collective-permute-start(bf16[4,4,72,512]{3,2,1,0:T(8,128)(2,1)S(1)} %place_pieces.8.own_ref), channel_id=1, source_target_pairs={{0,32},{1,9},{2,34},{3,11},{4,36},{5,13},{6,38},{7,15},{8,40},{9,1... | collective-permute-start | bytes 3538952 | tf_op jit(solution)/shard_map/ppermute | solution.py:138
  52.4 33.5 %collective-permute-start.11 = (bf16[4,4,72,512]{3,2,1,0:T(8,128)(2,1)S(1)}, bf16[4,4,72,512]{3,2,1,0:T(8,128)(2,1)S(1)}, u32[]{:S(2)}, u32[]{:S(2)}) collective-permute-start(bf16[4,4,72,512]{3,2,1,0:T(8,128)(2,1)S(1)} %place_pieces.8.own_ref), channel_id=1, source_target_pairs={{0,64},{1,17},{2,66},{3,19},{4,68},{5,21},{6,70},{7,23},{8,72},{9,... | collective-permute-start | bytes 3538952 | tf_op jit(solution)/shard_map/ppermute | solution.py:138
  55.0 30.9 %collective-permute-start.10 = (bf16[4,4,72,512]{3,2,1,0:T(8,128)(2,1)S(1)}, bf16[4,4,72,512]{3,2,1,0:T(8,128)(2,1)S(1)}, u32[]{:S(2)}, u32[]{:S(2)}) collective-permute-start(bf16[4,4,72,512]{3,2,1,0:T(8,128)(2,1)S(1)} %place_pieces.8.own_ref), channel_id=1, source_target_pairs={{0,96},{1,25},{2,98},{3,27},{4,100},{5,29},{6,102},{7,31},{8,104},... | collective-permute-start | bytes 3538952 | tf_op jit(solution)/shard_map/ppermute | solution.py:138
  90.6 38.0 %collective-permute-start.18 = (bf16[4,4,64,512]{3,2,1,0:T(8,128)(2,1)}, bf16[4,4,64,512]{3,2,1,0:T(8,128)(2,1)}, u32[]{:S(2)}, u32[]{:S(2)}) collective-permute-start(bf16[4,4,64,512]{3,2,1,0:T(8,128)(2,1)} %place_pieces.10.own_ref), channel_id=1, source_target_pairs={{0,32},{1,9},{2,34},{3,11},{4,36},{5,13},{6,38},{7,15},{8,40},{9,1... | collective-permute-start | bytes 3145736 | tf_op jit(solution)/shard_map/ppermute | solution.py:138
  91.5 48.7 %collective-permute-start.17 = (bf16[4,4,64,512]{3,2,1,0:T(8,128)(2,1)}, bf16[4,4,64,512]{3,2,1,0:T(8,128)(2,1)}, u32[]{:S(2)}, u32[]{:S(2)}) collective-permute-start(bf16[4,4,64,512]{3,2,1,0:T(8,128)(2,1)} %place_pieces.10.own_ref), channel_id=1, source_target_pairs={{0,64},{1,17},{2,66},{3,19},{4,68},{5,21},{6,70},{7,23},{8,72},{9,... | collective-permute-start | bytes 3145736 | tf_op jit(solution)/shard_map/ppermute | solution.py:138
  93.9 46.3 %collective-permute-start.16 = (bf16[4,4,64,512]{3,2,1,0:T(8,128)(2,1)}, bf16[4,4,64,512]{3,2,1,0:T(8,128)(2,1)}, u32[]{:S(2)}, u32[]{:S(2)}) collective-permute-start(bf16[4,4,64,512]{3,2,1,0:T(8,128)(2,1)} %place_pieces.10.own_ref), channel_id=1, source_target_pairs={{0,96},{1,25},{2,98},{3,27},{4,100},{5,29},{6,102},{7,31},{8,104},... | collective-permute-start | bytes 3145736 | tf_op jit(solution)/shard_map/ppermute | solution.py:138
  120.6 27.5 %collective-permute-start.14 = (bf16[512,512]{1,0:T(8,128)(2,1)}, bf16[512,512]{1,0:T(8,128)(2,1)S(1)}, u32[]{:S(2)}, u32[]{:S(2)}) collective-permute-start(bf16[512,512]{1,0:T(8,128)(2,1)} %get-tuple-element.62.att_ref.refs_0_), channel_id=1, source_target_pairs={{0,1},{1,0},{2,3},{3,2},{4,5},{5,4},{6,7},{7,6},{8,9},{9,8},{10,11... | collective-permute-start | bytes 1572872 | tf_op jit(solution)/shard_map/ppermute | solution.py:124
  176.9 4.3 collective-permute-start.20
  227.2 43.6 %collective-permute-start.22 = (bf16[4,4,88,512]{3,2,1,0:T(8,128)(2,1)}, bf16[4,4,88,512]{3,2,1,0:T(8,128)(2,1)S(1)}, u32[]{:S(2)}, u32[]{:S(2)}) collective-permute-start(bf16[4,4,88,512]{3,2,1,0:T(8,128)(2,1)} %get-tuple-element.80), channel_id=1, source_target_pairs={{0,32},{1,9},{2,34},{3,11},{4,36},{5,13},{6,38},{7,15},{8,40},{9,1... | collective-permute-start | bytes 4325384 | tf_op jit(solution)/shard_map/ppermute | solution.py:138
  227.3 43.5 %collective-permute-start.23 = (bf16[4,4,88,512]{3,2,1,0:T(8,128)(2,1)}, bf16[4,4,88,512]{3,2,1,0:T(8,128)(2,1)S(1)}, u32[]{:S(2)}, u32[]{:S(2)}) collective-permute-start(bf16[4,4,88,512]{3,2,1,0:T(8,128)(2,1)} %get-tuple-element.81), channel_id=1, source_target_pairs={{0,96},{1,25},{2,98},{3,27},{4,100},{5,29},{6,102},{7,31},{8,104},... | collective-permute-start | bytes 4325384 | tf_op jit(solution)/shard_map/ppermute | solution.py:138
  230.0 40.9 %collective-permute-start.24 = (bf16[4,4,88,512]{3,2,1,0:T(8,128)(2,1)}, bf16[4,4,88,512]{3,2,1,0:T(8,128)(2,1)}, u32[]{:S(2)}, u32[]{:S(2)}) collective-permute-start(bf16[4,4,88,512]{3,2,1,0:T(8,128)(2,1)} %get-tuple-element.82), channel_id=1, source_target_pairs={{0,64},{1,17},{2,66},{3,19},{4,68},{5,21},{6,70},{7,23},{8,72},{9,... | collective-permute-start | bytes 4325384 | tf_op jit(solution)/shard_map/ppermute | solution.py:138
  274.7 9.0 %collective-permute-start.25 = (bf16[4,88,512]{2,1,0:T(8,128)(2,1)S(1)}, bf16[4,88,512]{2,1,0:T(8,128)(2,1)S(1)}, u32[]{:S(2)}, u32[]{:S(2)}) collective-permute-start(bf16[4,88,512]{2,1,0:T(8,128)(2,1)S(1)} %get-tuple-element.84), channel_id=1, source_target_pairs={{0,8},{1,3},{2,10},{3,5},{4,12},{5,7},{6,14},{7,1},{8,16},{9,11},{... | collective-permute-start | bytes 1081352 | tf_op jit(solution)/shard_map/ppermute | solution.py:138
  276.1 7.5 %collective-permute-start.26 = (bf16[4,88,512]{2,1,0:T(8,128)(2,1)S(1)}, bf16[4,88,512]{2,1,0:T(8,128)(2,1)S(1)}, u32[]{:S(2)}, u32[]{:S(2)}) collective-permute-start(bf16[4,88,512]{2,1,0:T(8,128)(2,1)S(1)} %get-tuple-element.85), channel_id=1, source_target_pairs={{0,24},{1,7},{2,26},{3,1},{4,28},{5,3},{6,30},{7,5},{8,0},{9,15},{... | collective-permute-start | bytes 1081352 | tf_op jit(solution)/shard_map/ppermute | solution.py:138
  277.5 10.3 %collective-permute-start.27 = (bf16[4,88,512]{2,1,0:T(8,128)(2,1)S(1)}, bf16[4,88,512]{2,1,0:T(8,128)(2,1)S(1)}, u32[]{:S(2)}, u32[]{:S(2)}) collective-permute-start(bf16[4,88,512]{2,1,0:T(8,128)(2,1)S(1)} %get-tuple-element.86), channel_id=1, source_target_pairs={{0,16},{1,5},{2,18},{3,7},{4,20},{5,1},{6,22},{7,3},{8,24},{9,13},... | collective-permute-start | bytes 1081352 | tf_op jit(solution)/shard_map/ppermute | solution.py:138
  280.2 53.7 %collective-permute-start.19 = (f32[256,1024]{1,0:T(8,128)}, f32[256,1024]{1,0:T(8,128)}, u32[]{:S(2)}, u32[]{:S(2)}) collective-permute-start(f32[256,1024]{1,0:T(8,128)} %constant_dynamic-slice_fusion.4), channel_id=1, source_target_pairs={{0,1},{1,0},{2,3},{3,2},{4,5},{5,4},{6,7},{7,6},{8,9},{9,8},{10,11... | collective-permute-start | bytes 3145736 | tf_op jit(solution)/shard_map/ppermute | solution.py:124
  289.0 4.8 %collective-permute-start.28 = (bf16[88,512]{1,0:T(8,128)(2,1)S(1)}, bf16[88,512]{1,0:T(8,128)(2,1)S(1)}, u32[]{:S(2)}, u32[]{:S(2)}) collective-permute-start(bf16[88,512]{1,0:T(8,128)(2,1)S(1)} %get-tuple-element.88), channel_id=1, source_target_pairs={{0,2},{1,33},{2,4},{3,35},{4,6},{5,37},{6,0},{7,39},{8,10},{9,41},... | collective-permute-start | bytes 270344 | tf_op jit(solution)/shard_map/ppermute | solution.py:138
  290.1 3.8 collective-permute-start.29
  291.8 5.2 %collective-permute-start.30 = (bf16[88,512]{1,0:T(8,128)(2,1)S(1)}, bf16[88,512]{1,0:T(8,128)(2,1)S(1)}, u32[]{:S(2)}, u32[]{:S(2)}) collective-permute-start(bf16[88,512]{1,0:T(8,128)(2,1)S(1)} %get-tuple-element.90), channel_id=1, source_target_pairs={{0,4},{1,65},{2,6},{3,67},{4,0},{5,69},{6,2},{7,71},{8,12},{9,73},... | collective-permute-start | bytes 270344 | tf_op jit(solution)/shard_map/ppermute | solution.py:138
  297.1 4.2 collective-permute-start.31
  301.5 5.5 %collective-permute-start.34 = (bf16[88,512]{1,0:T(8,128)(2,1)S(1)}, bf16[88,512]{1,0:T(8,128)(2,1)S(1)}, u32[]{:S(2)}, u32[]{:S(2)}) collective-permute-start(bf16[88,512]{1,0:T(8,128)(2,1)S(1)} %pad_maximum_fusion.1.own_ref), channel_id=1, source_target_pairs={{0,2},{1,33},{2,4},{3,35},{4,6},{5,37},{6,0},{7,39},{8,10},{9,41},... | collective-permute-start | bytes 270344 | tf_op jit(solution)/shard_map/ppermute | solution.py:138
  302.8 4.9 %collective-permute-start.33 = (bf16[88,512]{1,0:T(8,128)(2,1)S(1)}, bf16[88,512]{1,0:T(8,128)(2,1)S(1)}, u32[]{:S(2)}, u32[]{:S(2)}) collective-permute-start(bf16[88,512]{1,0:T(8,128)(2,1)S(1)} %pad_maximum_fusion.1.own_ref), channel_id=1, source_target_pairs={{0,4},{1,65},{2,6},{3,67},{4,0},{5,69},{6,2},{7,71},{8,12},{9,73},... | collective-permute-start | bytes 270344 | tf_op jit(solution)/shard_map/ppermute | solution.py:138
  304.4 3.9 collective-permute-start.32
  306.3 30.7 %collective-permute-start.21 = (f32[256,1024]{1,0:T(8,128)}, f32[256,1024]{1,0:T(8,128)}, u32[]{:S(2)}, u32[]{:S(2)}) collective-permute-start(f32[256,1024]{1,0:T(8,128)} %constant_dynamic-slice_fusion.3), channel_id=1, source_target_pairs={{0,1},{1,0},{2,3},{3,2},{4,5},{5,4},{6,7},{7,6},{8,9},{9,8},{10,11... | collective-permute-start | bytes 3145736 | tf_op jit(solution)/shard_map/ppermute | solution.py:124
  309.4 12.4 %collective-permute-start.37 = (bf16[4,88,512]{2,1,0:T(8,128)(2,1)S(1)}, bf16[4,88,512]{2,1,0:T(8,128)(2,1)S(1)}, u32[]{:S(2)}, u32[]{:S(2)}) collective-permute-start(bf16[4,88,512]{2,1,0:T(8,128)(2,1)S(1)} %place_pieces.12.own_ref), channel_id=1, source_target_pairs={{0,8},{1,3},{2,10},{3,5},{4,12},{5,7},{6,14},{7,1},{8,16},{9,11},{... | collective-permute-start | bytes 1081352 | tf_op jit(solution)/shard_map/ppermute | solution.py:138
  309.5 16.7 %collective-permute-start.36 = (bf16[4,88,512]{2,1,0:T(8,128)(2,1)S(1)}, bf16[4,88,512]{2,1,0:T(8,128)(2,1)S(1)}, u32[]{:S(2)}, u32[]{:S(2)}) collective-permute-start(bf16[4,88,512]{2,1,0:T(8,128)(2,1)S(1)} %place_pieces.12.own_ref), channel_id=1, source_target_pairs={{0,16},{1,5},{2,18},{3,7},{4,20},{5,1},{6,22},{7,3},{8,24},{9,13},... | collective-permute-start | bytes 1081352 | tf_op jit(solution)/shard_map/ppermute | solution.py:138
  311.5 15.0 %collective-permute-start.35 = (bf16[4,88,512]{2,1,0:T(8,128)(2,1)S(1)}, bf16[4,88,512]{2,1,0:T(8,128)(2,1)S(1)}, u32[]{:S(2)}, u32[]{:S(2)}) collective-permute-start(bf16[4,88,512]{2,1,0:T(8,128)(2,1)S(1)} %place_pieces.12.own_ref), channel_id=1, source_target_pairs={{0,24},{1,7},{2,26},{3,1},{4,28},{5,3},{6,30},{7,5},{8,0},{9,15},{... | collective-permute-start | bytes 1081352 | tf_op jit(solution)/shard_map/ppermute | solution.py:138
  317.0 15.0 %copy-start.19 = (bf16[128,3072]{1,0:T(8,128)(2,1)S(1)}, bf16[128,3072]{1,0:T(8,128)(2,1)}, u32[]{:S(2)}) copy-start(bf16[128,3072]{1,0:T(8,128)(2,1)} %copy-done.18) | copy-start | bytes 2359300
  327.3 32.8 %collective-permute-start.40 = (bf16[4,4,88,512]{3,2,1,0:T(8,128)(2,1)S(1)}, bf16[4,4,88,512]{3,2,1,0:T(8,128)(2,1)S(1)}, u32[]{:S(2)}, u32[]{:S(2)}) collective-permute-start(bf16[4,4,88,512]{3,2,1,0:T(8,128)(2,1)S(1)} %place_pieces.13.own_ref), channel_id=1, source_target_pairs={{0,32},{1,9},{2,34},{3,11},{4,36},{5,13},{6,38},{7,15},{8,40},{9,1... | collective-permute-start | bytes 4325384 | tf_op jit(solution)/shard_map/ppermute | solution.py:138
  328.1 63.4 %collective-permute-start.39 = (bf16[4,4,88,512]{3,2,1,0:T(8,128)(2,1)S(1)}, bf16[4,4,88,512]{3,2,1,0:T(8,128)(2,1)S(1)}, u32[]{:S(2)}, u32[]{:S(2)}) collective-permute-start(bf16[4,4,88,512]{3,2,1,0:T(8,128)(2,1)S(1)} %place_pieces.13.own_ref), channel_id=1, source_target_pairs={{0,64},{1,17},{2,66},{3,19},{4,68},{5,21},{6,70},{7,23},{8,72},{9,... | collective-permute-start | bytes 4325384 | tf_op jit(solution)/shard_map/ppermute | solution.py:138
  331.7 62.7 %collective-permute-start.38 = (bf16[4,4,88,512]{3,2,1,0:T(8,128)(2,1)S(1)}, bf16[4,4,88,512]{3,2,1,0:T(8,128)(2,1)}, u32[]{:S(2)}, u32[]{:S(2)}) collective-permute-start(bf16[4,4,88,512]{3,2,1,0:T(8,128)(2,1)S(1)} %place_pieces.13.own_ref), channel_id=1, source_target_pairs={{0,96},{1,25},{2,98},{3,27},{4,100},{5,29},{6,102},{7,31},{8,104},... | collective-permute-start | bytes 4325384 | tf_op jit(solution)/shard_map/ppermute | solution.py:138
  360.1 34.3 %copy-start.25 = (bf16[4,4,88,512]{3,2,1,0:T(8,128)(2,1)}, bf16[4,4,88,512]{3,2,1,0:T(8,128)(2,1)S(1)}, u32[]{:S(2)}) copy-start(bf16[4,4,88,512]{3,2,1,0:T(8,128)(2,1)S(1)} %collective-permute-done.40.prev_ref) | copy-start | bytes 4325380
  404.6 18.6 %collective-permute-start.41 = (bf16[1024,1024]{1,0:T(8,128)(2,1)}, bf16[1024,1024]{1,0:T(8,128)(2,1)S(1)}, u32[]{:S(2)}, u32[]{:S(2)}) collective-permute-start(bf16[1024,1024]{1,0:T(8,128)(2,1)} %other_half.1), channel_id=1, source_target_pairs={{0,1},{1,0},{2,3},{3,2},{4,5},{5,4},{6,7},{7,6},{8,9},{9,8},{10,11... | collective-permute-start | bytes 6291464 | tf_op jit(solution)/shard_map/ppermute | solution.py:124
  (30 other events, 159.8 us)
Sparse Core Ops, SparseCore 0:
  12.0 122.5 all-gather.1
  175.5 223.8 all-reduce.1
